TPU v7x, 512 devices: a whole 4x4x16 slice. The times are simulated.
512 devices in a mesh: ctx: 64 (over z_lo, y, core), head: 8 (over x, z_hi).
Axes of the slice: x: 4, y: 4, z: 16 (z_hi: 2, z_lo: 8; z = z_hi * 8 + z_lo), core: 2. Of those that a mesh axis runs over, the one named last changes fastest.
Arguments:
- block_order: int32 [64], P('ctx'), may hold values from 0 to 63, as said below
- query_b: bfloat16 [16384, 32, 128], P('ctx', 'head'), may hold values from -6 to 6
- key_b: bfloat16 [16384, 8, 128], P('ctx', 'head'), may hold values from -6 to 6
- value_b: bfloat16 [16384, 8, 128], P('ctx', 'head'), may hold values from -6 to 6
- out_weight: bfloat16 [32, 128, 4096], P('head', None, 'ctx'), may hold values from -0.1875 to 0.1875
- query_a: bfloat16 [16384, 32, 128], P('ctx', 'head'), may hold values from -6 to 6
- key_a: bfloat16 [16384, 8, 128], P('ctx', 'head'), may hold values from -6 to 6
- value_a: bfloat16 [16384, 8, 128], P('ctx', 'head'), may hold values from -6 to 6
- grad_a: bfloat16 [16384, 32, 128], P('ctx', 'head'), may hold values from -6 to 6
Outputs:
- out_b: bfloat16 [16384, 4096], P('ctx', 'head')
- grad_query_a: bfloat16 [16384, 32, 128], P('ctx', 'head')
- grad_key_a: bfloat16 [16384, 8, 128], P('ctx', 'head')
- grad_value_a: bfloat16 [16384, 8, 128], P('ctx', 'head')
Inputs may be any that keep to these rules, and one draw needn't show every extreme that they name: block_order[p] = (p - c) mod (64) for one offset c: cycle neighbours hold neighbouring sequence blocks, and the sequence begins at cycle position c.
All inputs are finite; a program needn't handle non-finite values.
Results may differ from a plain program's by a relative error of at most 0.019.
Values may be sent and summed in bfloat16 or wider, within the bound.
A program may use at most 64 MiB of HBM per device.

v0:
```python
import jax
import jax.numpy as jnp
from jax import lax
from jax.sharding import PartitionSpec as P

HOPS = 4


def from_behind(x, axis, by):
    devices = lax.axis_size(axis)
    return lax.ppermute(x, axis, [(i, (i + by) % devices) for i in range(devices)])


def split_heads(array, kv_count):
    row_count, head_count, head_dim = array.shape
    return array.reshape(row_count, kv_count, head_count // kv_count, head_dim)


def tile_scores(query4, key_rows, query_pos, key_block):
    row_count = key_rows.shape[0]
    score_scale = query4.shape[-1] ** (-0.5)
    scores = (
        jnp.einsum("rkgd,ckd->kgrc", query4, key_rows, preferred_element_type=jnp.float32)
        * score_scale
    )
    key_pos = key_block * row_count + jnp.arange(row_count, dtype=jnp.int32)
    distance = query_pos[:, None] - key_pos[None, :]
    allowed = (distance >= 0) & (distance < HOPS * row_count)
    return jnp.where(allowed, scores, -jnp.inf)


def start_state(query4):
    stat_shape = (query4.shape[1], query4.shape[2], query4.shape[0])
    return (
        jnp.full(stat_shape, -jnp.inf, jnp.float32),
        jnp.zeros(stat_shape, jnp.float32),
        jnp.zeros(stat_shape + (query4.shape[3],), jnp.float32),
    )


def absorb(running, query4, key_rows, value_rows, query_pos, key_block):
    running_max, totals, weighted = running
    scores = tile_scores(query4, key_rows, query_pos, key_block)
    new_max = jnp.maximum(running_max, jnp.max(scores, axis=-1))
    factor = jnp.exp(running_max - new_max)
    powers = jnp.exp(scores - new_max[..., None])
    totals = totals * factor + jnp.sum(powers, axis=-1)
    weighted = weighted * factor[..., None] + jnp.einsum(
        "kgrc,ckd->kgrd",
        powers.astype(jnp.bfloat16),
        value_rows,
        preferred_element_type=jnp.float32,
    )
    return (new_max, totals, weighted)


def tile_gradients(query4, grad4, key_rows, value_rows, query_pos, key_block, log_totals, deltas):
    score_scale = query4.shape[-1] ** (-0.5)
    scores = tile_scores(query4, key_rows, query_pos, key_block)
    probs = jnp.exp(scores - log_totals[..., None])
    part_values = jnp.einsum(
        "kgrc,rkgd->ckd", probs.astype(jnp.bfloat16), grad4, preferred_element_type=jnp.float32
    )
    grad_probs = jnp.einsum("rkgd,ckd->kgrc", grad4, value_rows, preferred_element_type=jnp.float32)
    grad_scores = (probs * (grad_probs - deltas[..., None])).astype(jnp.bfloat16)
    part_query = (
        jnp.einsum("kgrc,ckd->rkgd", grad_scores, key_rows, preferred_element_type=jnp.float32)
        * score_scale
    )
    part_keys = (
        jnp.einsum("kgrc,rkgd->ckd", grad_scores, query4, preferred_element_type=jnp.float32)
        * score_scale
    )
    return (part_query, part_keys, part_values)


def local(block_order, query_b, key_b, value_b, out_weight, query_a, key_a, value_a, grad_a):
    row_count = query_b.shape[0]
    kv_count = key_b.shape[1]
    head_dim = query_b.shape[2]
    cycle_size = lax.axis_size("ctx")
    own_block = block_order[0]
    query_pos = own_block * row_count + jnp.arange(row_count, dtype=jnp.int32)
    query_b4 = split_heads(query_b, kv_count)
    query_a4 = split_heads(query_a, kv_count)
    grad_a4 = split_heads(grad_a, kv_count)
    initial = start_state(query_b4)
    state_b = absorb(initial, query_b4, key_b, value_b, query_pos, own_block)
    state_a = absorb(initial, query_a4, key_a, value_a, query_pos, own_block)
    kept_blocks = []
    moving_keys, moving_values = (key_b, value_b)
    for hop_index in range(HOPS):
        moving_keys, moving_values = from_behind((moving_keys, moving_values), "ctx", 1)
        key_block = (own_block - hop_index - 1) % cycle_size
        state_b = absorb(state_b, query_b4, moving_keys, moving_values, query_pos, key_block)
    moving_keys, moving_values = (key_a, value_a)
    for hop_index in range(HOPS):
        moving_keys, moving_values = from_behind((moving_keys, moving_values), "ctx", 1)
        key_block = (own_block - hop_index - 1) % cycle_size
        state_a = absorb(state_a, query_a4, moving_keys, moving_values, query_pos, key_block)
        kept_blocks.append((moving_keys, moving_values))
    attended = (state_b[2] / state_b[1][..., None]).astype(jnp.bfloat16)
    weight_piece = lax.all_gather(out_weight, "ctx", axis=2, tiled=True)
    weight4 = weight_piece.reshape(
        kv_count, weight_piece.shape[0] // kv_count, weight_piece.shape[1], weight_piece.shape[2]
    )
    partial_terms = jnp.einsum(
        "kgrd,kgdn->rn", attended, weight4, preferred_element_type=jnp.float32
    )
    out_b = lax.psum_scatter(
        partial_terms.astype(jnp.bfloat16), "head", scatter_dimension=1, tiled=True
    )
    top_a, totals_a, weighted_a = state_a
    outputs_a = weighted_a / totals_a[..., None]
    log_totals = top_a + jnp.log(totals_a)
    deltas = jnp.sum(jnp.transpose(grad_a4, (1, 2, 0, 3)).astype(jnp.float32) * outputs_a, axis=-1)
    grad_query, grad_keys, grad_values = tile_gradients(
        query_a4, grad_a4, key_a, value_a, query_pos, own_block, log_totals, deltas
    )
    moving_keys, moving_values = (key_a, value_a)
    sum_keys, sum_values = (grad_keys, grad_values)
    for hop_index in range(HOPS):
        moving_keys, moving_values = from_behind((moving_keys, moving_values), "ctx", 1)
        sum_keys, sum_values = (
            from_behind(sum_keys.astype(jnp.bfloat16), "ctx", 1).astype(sum_keys.dtype),
            from_behind(sum_values.astype(jnp.bfloat16), "ctx", 1).astype(sum_values.dtype),
        )
        key_block = (own_block - hop_index - 1) % cycle_size
        part_query, part_keys, part_values = tile_gradients(
            query_a4, grad_a4, moving_keys, moving_values, query_pos, key_block, log_totals, deltas
        )
        grad_query = grad_query + part_query
        sum_keys = sum_keys + part_keys
        sum_values = sum_values + part_values
    grad_keys, grad_values = (
        from_behind(sum_keys.astype(jnp.bfloat16), "ctx", -HOPS).astype(sum_keys.dtype),
        from_behind(sum_values.astype(jnp.bfloat16), "ctx", -HOPS).astype(sum_values.dtype),
    )
    grad_query_a = grad_query.reshape(row_count, -1, head_dim).astype(jnp.bfloat16)
    return (out_b, grad_query_a, grad_keys.astype(jnp.bfloat16), grad_values.astype(jnp.bfloat16))


def solution(mesh):
    placed = (
        P("ctx"),
        P("ctx", "head", None),
        P("ctx", "head", None),
        P("ctx", "head", None),
        P("head", None, "ctx"),
        P("ctx", "head", None),
        P("ctx", "head", None),
        P("ctx", "head", None),
        P("ctx", "head", None),
    )
    return jax.shard_map(
        local,
        mesh=mesh,
        in_specs=placed,
        out_specs=(
            P("ctx", "head"),
            P("ctx", "head", None),
            P("ctx", "head", None),
            P("ctx", "head", None),
        ),
        check_vma=False,
    )
```

profile of v0, /device:TPU:1, one launch (start us, length us, event | category | flops | bytes accessed | tf_op | source)
XLA Modules:
  0.0 305.7 jit_solution(6303813950112833167)
XLA Ops:
  7.2 4.7 %collective-permute-start.8 = (bf16[256,1,128]{2,0,1:T(8,128)(2,1)}, bf16[256,1,128]{2,0,1:T(8,128)(2,1)S(1)}, u32[]{:S(2)}, u32[]{:S(2)}) collective-permute-start(bf16[256,1,128]{2,0,1:T(8,128)(2,1)} %param.15), channel_id=1, source_target_pairs={{0,8},{8,16},{16,24},{24,32},{32,40},{40,48},{48,56},{56,64},{64,7... | collective-permute-start | bytes 196616 | tf_op jit(solution)/shard_map/ppermute | solution.py:11
  12.0 0.9 copy.27
  12.9 1.9 collective-permute-start.12
  14.9 3.6 %collective-permute-start = (bf16[256,1,128]{2,0,1:T(8,128)(2,1)}, bf16[256,1,128]{2,0,1:T(8,128)(2,1)S(1)}, u32[]{:S(2)}, u32[]{:S(2)}) collective-permute-start(bf16[256,1,128]{2,0,1:T(8,128)(2,1)} %param.11), channel_id=1, source_target_pairs={{0,8},{8,16},{16,24},{24,32},{32,40},{40,48},{48,56},{56,64},{64,7... | collective-permute-start | bytes 196616 | tf_op jit(solution)/shard_map/ppermute | solution.py:11
  18.5 1.9 collective-permute-start.1
  21.6 1.2 fusion.203
  22.8 1.6 fusion.198
  24.3 0.9 fusion.82
  25.7 3.3 %collective-permute-start.9 = (bf16[256,1,128]{2,0,1:T(8,128)(2,1)S(1)}, bf16[256,1,128]{2,0,1:T(8,128)(2,1)S(1)}, u32[]{:S(2)}, u32[]{:S(2)}) collective-permute-start(bf16[256,1,128]{2,0,1:T(8,128)(2,1)S(1)} %collective-permute-done.8), channel_id=1, source_target_pairs={{0,8},{8,16},{16,24},{24,32},{32,40},{40,48},{48,56},{56,64},{64,7... | collective-permute-start | bytes 196616 | tf_op jit(solution)/shard_map/ppermute | solution.py:11
  29.0 1.9 collective-permute-start.2
  31.6 3.6 %collective-permute-start.13 = (bf16[256,1,128]{0,2,1:T(8,128)(2,1)S(1)}, bf16[256,1,128]{0,2,1:T(8,128)(2,1)S(1)}, u32[]{:S(2)}, u32[]{:S(2)}) collective-permute-start(bf16[256,1,128]{0,2,1:T(8,128)(2,1)S(1)} %collective-permute-done.12), channel_id=1, source_target_pairs={{0,8},{8,16},{16,24},{24,32},{32,40},{40,48},{48,56},{56,64},{64,7... | collective-permute-start | bytes 196616 | tf_op jit(solution)/shard_map/ppermute | solution.py:11
  35.2 1.9 collective-permute-start.3
  37.1 3.6 %collective-permute-start.10 = (bf16[256,1,128]{2,0,1:T(8,128)(2,1)S(1)}, bf16[256,1,128]{2,0,1:T(8,128)(2,1)S(1)}, u32[]{:S(2)}, u32[]{:S(2)}) collective-permute-start(bf16[256,1,128]{2,0,1:T(8,128)(2,1)S(1)} %collective-permute-done.9), channel_id=1, source_target_pairs={{0,8},{8,16},{16,24},{24,32},{32,40},{40,48},{48,56},{56,64},{64,7... | collective-permute-start | bytes 196616 | tf_op jit(solution)/shard_map/ppermute | solution.py:11
  40.7 1.9 collective-permute-start.4
  43.3 3.6 %collective-permute-start.14 = (bf16[256,1,128]{0,2,1:T(8,128)(2,1)S(1)}, bf16[256,1,128]{0,2,1:T(8,128)(2,1)S(1)}, u32[]{:S(2)}, u32[]{:S(2)}) collective-permute-start(bf16[256,1,128]{0,2,1:T(8,128)(2,1)S(1)} %collective-permute-done.13), channel_id=1, source_target_pairs={{0,8},{8,16},{16,24},{24,32},{32,40},{40,48},{48,56},{56,64},{64,7... | collective-permute-start | bytes 196616 | tf_op jit(solution)/shard_map/ppermute | solution.py:11
  46.9 1.9 collective-permute-start.5
  48.9 3.3 %collective-permute-start.11 = (bf16[256,1,128]{2,0,1:T(8,128)(2,1)S(1)}, bf16[256,1,128]{2,0,1:T(8,128)(2,1)S(1)}, u32[]{:S(2)}, u32[]{:S(2)}) collective-permute-start(bf16[256,1,128]{2,0,1:T(8,128)(2,1)S(1)} %collective-permute-done.10), channel_id=1, source_target_pairs={{0,8},{8,16},{16,24},{24,32},{32,40},{40,48},{48,56},{56,64},{64,7... | collective-permute-start | bytes 196616 | tf_op jit(solution)/shard_map/ppermute | solution.py:11
  52.2 1.9 collective-permute-start.6
  54.8 3.6 %collective-permute-start.15 = (bf16[256,1,128]{0,2,1:T(8,128)(2,1)S(1)}, bf16[256,1,128]{0,2,1:T(8,128)(2,1)S(1)}, u32[]{:S(2)}, u32[]{:S(2)}) collective-permute-start(bf16[256,1,128]{0,2,1:T(8,128)(2,1)S(1)} %collective-permute-done.14), channel_id=1, source_target_pairs={{0,8},{8,16},{16,24},{24,32},{32,40},{40,48},{48,56},{56,64},{64,7... | collective-permute-start | bytes 196616 | tf_op jit(solution)/shard_map/ppermute | solution.py:11
  58.4 1.9 collective-permute-start.7
  61.4 0.9 fusion.69
  62.4 3.6 %collective-permute-start.21 = (bf16[256,1,128]{2,0,1:T(8,128)(2,1)}, bf16[256,1,128]{2,0,1:T(8,128)(2,1)}, u32[]{:S(2)}, u32[]{:S(2)}) collective-permute-start(bf16[256,1,128]{2,0,1:T(8,128)(2,1)} %fusion.69), channel_id=1, source_target_pairs={{0,8},{8,16},{16,24},{24,32},{32,40},{40,48},{48,56},{56,64},{64,7... | collective-permute-start | bytes 196616 | tf_op jit(solution)/shard_map/ppermute | solution.py:11
  68.8 0.9 fusion.70
  69.7 2.1 collective-permute-start.16
  72.9 1.1 fusion.37
  74.7 1.1 fusion.40
  76.5 1.2 fusion.51
  78.1 1.2 fusion.49
  79.6 67.5 %all-gather.2.cloned.1.call-done = bf16[4,128,4096]{1,2,0:T(8,128)(2,1)} async-done(((bf16[4,128,64]{1,2,0:T(8,128)(2,1)}), bf16[4,128,4096]{1,2,0:T(8,128)(2,1)}) %all-gather.2.cloned.1.call-update) | async-done | bytes 4194320 | tf_op jit(solution)/shard_map/all_gather | solution.py:103
  147.1 5.7 %fusion = bf16[256,4096]{1,0:T(8,128)(2,1)} fusion(bf16[4,128,4096]{1,2,0:T(8,128)(2,1)} %all-gather.2.cloned.1.call-done, f32[4,256,128]{2,1,0:T(8,128)} %fusion.49, f32[1,4,256,256]{2,3,1,0:T(8,128)} %copy-done.12, f32[4,256]{1,0:T(4,128)S(1)} %get-tuple-element.23, f32[4,256]{1,0:T(4,128)S(1)} %get-tuple-element.18, ...), kind=kOutput, calls=%fused_computation.1 | convolution fusion | flops 1142816768 | bytes 7938048 | tf_op jit(solution)/shard_map/kgrd,kgdn->rn/dot_general | solution.py:107
  153.2 1.6 fusion.172
  155.1 1.6 convolution_bitcast_fusion.7
  158.5 1.1 add_convert_fusion.3
  159.6 2.0 collective-permute-start.22
  161.6 1.1 add_convert_fusion.7
  162.7 2.2 collective-permute-start.17
  164.9 2.7 collective-permute-start.23
  167.7 2.8 collective-permute-start.18
  170.5 6.5 %collective-permute-done.23 = bf16[256,1,128]{2,0,1:T(8,128)(2,1)S(1)} collective-permute-done((bf16[256,1,128]{2,0,1:T(8,128)(2,1)S(1)}, bf16[256,1,128]{2,0,1:T(8,128)(2,1)S(1)}, u32[]{:S(2)}, u32[]{:S(2)}) %collective-permute-start.23) | collective-permute-done | bytes 65568 | tf_op jit(solution)/shard_map/ppermute | solution.py:11
  177.1 1.9 collective-permute-start.24
  179.0 2.7 collective-permute-done.18
  181.7 1.9 collective-permute-start.19
  183.6 7.7 %collective-permute-done.24 = bf16[256,1,128]{2,0,1:T(8,128)(2,1)S(1)} collective-permute-done((bf16[256,1,128]{2,0,1:T(8,128)(2,1)S(1)}, bf16[256,1,128]{2,0,1:T(8,128)(2,1)S(1)}, u32[]{:S(2)}, u32[]{:S(2)}) %collective-permute-start.24) | collective-permute-done | bytes 65568 | tf_op jit(solution)/shard_map/ppermute | solution.py:11
  191.4 7.1 %collective-permute-start.25 = (bf16[256,1,128]{2,0,1:T(8,128)(2,1)S(1)}, bf16[256,1,128]{2,0,1:T(8,128)(2,1)S(1)}, u32[]{:S(2)}, u32[]{:S(2)}) collective-permute-start(bf16[256,1,128]{2,0,1:T(8,128)(2,1)S(1)} %add_convert_fusion), channel_id=1, source_target_pairs={{0,480},{8,488},{16,496},{24,504},{32,0},{40,8},{48,16},{56,24},{6... | collective-permute-start | bytes 196616 | tf_op jit(solution)/shard_map/ppermute | solution.py:11
  198.5 1.9 collective-permute-start.20
  201.7 1.6 collective-permute-done.25
  203.3 9.6 %collective-permute-done.20 = bf16[256,1,128]{2,0,1:T(8,128)(2,1)S(1)} collective-permute-done((bf16[256,1,128]{2,0,1:T(8,128)(2,1)S(1)}, bf16[256,1,128]{2,0,1:T(8,128)(2,1)S(1)}, u32[]{:S(2)}, u32[]{:S(2)}) %collective-permute-start.20) | collective-permute-done | bytes 65568 | tf_op jit(solution)/shard_map/ppermute | solution.py:11
  212.9 84.7 %reduce-scatter.2.cloned.1.call-done = bf16[256,512]{1,0:T(8,128)(2,1)} async-done(((bf16[256,4096]{1,0:T(8,128)(2,1)}), bf16[256,512]{1,0:T(8,128)(2,1)}) %reduce-scatter.2.cloned.1.call-update) | async-done | bytes 262160 | tf_op jit(solution)/shard_map/reduce_scatter | solution.py:110
  (131 shorter events, 14.6 us)
Async XLA Ops:
  7.2 14.4 %copy-start = (bf16[256,4,128]{2,1,0:T(4,128)(2,1)S(1)}, bf16[256,4,128]{2,1,0:T(4,128)(2,1)}, u32[]{:S(2)}) copy-start(bf16[256,4,128]{2,1,0:T(4,128)(2,1)} %param.14) | copy-start | bytes 786436
  7.2 24.0 %copy-start.8 = (bf16[256,4,128]{2,1,0:T(4,128)(2,1)S(1)}, bf16[256,4,128]{2,1,0:T(4,128)(2,1)}, u32[]{:S(2)}) copy-start(bf16[256,4,128]{2,1,0:T(4,128)(2,1)} %param.10) | copy-start | bytes 786436
  7.2 18.3 %copy-start.21 = (bf16[256,4,128]{2,1,0:T(4,128)(2,1)S(1)}, bf16[256,4,128]{2,1,0:T(4,128)(2,1)}, u32[]{:S(2)}) copy-start(bf16[256,4,128]{2,1,0:T(4,128)(2,1)} %param.17) | copy-start | bytes 786436
  7.2 139.9 %all-gather.2.cloned.1.call-start = ((), (), s32[]{:S(2)}) async-start(), calls=%async_computation.1 | async-start | bytes 4259840 | tf_op jit(solution)/shard_map/all_gather | solution.py:103
  7.2 18.4 %collective-permute-start.8 = (bf16[256,1,128]{2,0,1:T(8,128)(2,1)}, bf16[256,1,128]{2,0,1:T(8,128)(2,1)S(1)}, u32[]{:S(2)}, u32[]{:S(2)}) collective-permute-start(bf16[256,1,128]{2,0,1:T(8,128)(2,1)} %param.15), channel_id=1, source_target_pairs={{0,8},{8,16},{16,24},{24,32},{32,40},{40,48},{48,56},{56,64},{64,7... | collective-permute-start | bytes 196616 | tf_op jit(solution)/shard_map/ppermute | solution.py:11
  12.9 18.6 %collective-permute-start.12 = (bf16[256,1,128]{0,2,1:T(8,128)(2,1)S(1)}, bf16[256,1,128]{0,2,1:T(8,128)(2,1)S(1)}, u32[]{:S(2)}, u32[]{:S(2)}) collective-permute-start(bf16[256,1,128]{0,2,1:T(8,128)(2,1)S(1)} %copy.27), channel_id=1, source_target_pairs={{0,8},{8,16},{16,24},{24,32},{32,40},{40,48},{48,56},{56,64},{64,7... | collective-permute-start | bytes 196616 | tf_op jit(solution)/shard_map/ppermute | solution.py:11
  14.9 14.1 %collective-permute-start = (bf16[256,1,128]{2,0,1:T(8,128)(2,1)}, bf16[256,1,128]{2,0,1:T(8,128)(2,1)S(1)}, u32[]{:S(2)}, u32[]{:S(2)}) collective-permute-start(bf16[256,1,128]{2,0,1:T(8,128)(2,1)} %param.11), channel_id=1, source_target_pairs={{0,8},{8,16},{16,24},{24,32},{32,40},{40,48},{48,56},{56,64},{64,7... | collective-permute-start | bytes 196616 | tf_op jit(solution)/shard_map/ppermute | solution.py:11
  18.5 16.7 %collective-permute-start.1 = (bf16[256,1,128]{2,0,1:T(8,128)(2,1)}, bf16[256,1,128]{2,0,1:T(8,128)(2,1)}, u32[]{:S(2)}, u32[]{:S(2)}) collective-permute-start(bf16[256,1,128]{2,0,1:T(8,128)(2,1)} %param.12), channel_id=1, source_target_pairs={{0,8},{8,16},{16,24},{24,32},{32,40},{40,48},{48,56},{56,64},{64,7... | collective-permute-start | bytes 196616 | tf_op jit(solution)/shard_map/ppermute | solution.py:11
  20.4 277.2 %reduce-scatter.2.cloned.1.call-start = ((), (), s32[]{:S(2)}) async-start(), calls=%async_computation.2 | async-start | bytes 2359296 | tf_op jit(solution)/shard_map/reduce_scatter | solution.py:110
  25.7 11.4 %collective-permute-start.9 = (bf16[256,1,128]{2,0,1:T(8,128)(2,1)S(1)}, bf16[256,1,128]{2,0,1:T(8,128)(2,1)S(1)}, u32[]{:S(2)}, u32[]{:S(2)}) collective-permute-start(bf16[256,1,128]{2,0,1:T(8,128)(2,1)S(1)} %collective-permute-done.8), channel_id=1, source_target_pairs={{0,8},{8,16},{16,24},{24,32},{32,40},{40,48},{48,56},{56,64},{64,7... | collective-permute-start | bytes 196616 | tf_op jit(solution)/shard_map/ppermute | solution.py:11
  29.0 11.8 %collective-permute-start.2 = (bf16[256,1,128]{2,0,1:T(8,128)(2,1)S(1)}, bf16[256,1,128]{2,0,1:T(8,128)(2,1)S(1)}, u32[]{:S(2)}, u32[]{:S(2)}) collective-permute-start(bf16[256,1,128]{2,0,1:T(8,128)(2,1)S(1)} %collective-permute-done), channel_id=1, source_target_pairs={{0,8},{8,16},{16,24},{24,32},{32,40},{40,48},{48,56},{56,64},{64,7... | collective-permute-start | bytes 196616 | tf_op jit(solution)/shard_map/ppermute | solution.py:11
  31.6 11.7 %collective-permute-start.13 = (bf16[256,1,128]{0,2,1:T(8,128)(2,1)S(1)}, bf16[256,1,128]{0,2,1:T(8,128)(2,1)S(1)}, u32[]{:S(2)}, u32[]{:S(2)}) collective-permute-start(bf16[256,1,128]{0,2,1:T(8,128)(2,1)S(1)} %collective-permute-done.12), channel_id=1, source_target_pairs={{0,8},{8,16},{16,24},{24,32},{32,40},{40,48},{48,56},{56,64},{64,7... | collective-permute-start | bytes 196616 | tf_op jit(solution)/shard_map/ppermute | solution.py:11
  35.2 11.7 %collective-permute-start.3 = (bf16[256,1,128]{2,0,1:T(8,128)(2,1)}, bf16[256,1,128]{2,0,1:T(8,128)(2,1)S(1)}, u32[]{:S(2)}, u32[]{:S(2)}) collective-permute-start(bf16[256,1,128]{2,0,1:T(8,128)(2,1)} %collective-permute-done.1), channel_id=1, source_target_pairs={{0,8},{8,16},{16,24},{24,32},{32,40},{40,48},{48,56},{56,64},{64,7... | collective-permute-start | bytes 196616 | tf_op jit(solution)/shard_map/ppermute | solution.py:11
  37.1 23.9 %copy-start.17 = (bf16[256,1,128]{2,0,1:T(8,128)(2,1)}, bf16[256,1,128]{2,0,1:T(8,128)(2,1)S(1)}, u32[]{:S(2)}) copy-start(bf16[256,1,128]{2,0,1:T(8,128)(2,1)S(1)} %collective-permute-done.9) | copy-start | bytes 196612
  37.1 11.7 %collective-permute-start.10 = (bf16[256,1,128]{2,0,1:T(8,128)(2,1)S(1)}, bf16[256,1,128]{2,0,1:T(8,128)(2,1)S(1)}, u32[]{:S(2)}, u32[]{:S(2)}) collective-permute-start(bf16[256,1,128]{2,0,1:T(8,128)(2,1)S(1)} %collective-permute-done.9), channel_id=1, source_target_pairs={{0,8},{8,16},{16,24},{24,32},{32,40},{40,48},{48,56},{56,64},{64,7... | collective-permute-start | bytes 196616 | tf_op jit(solution)/shard_map/ppermute | solution.py:11
  40.7 11.4 %collective-permute-start.4 = (bf16[256,1,128]{2,0,1:T(8,128)(2,1)S(1)}, bf16[256,1,128]{2,0,1:T(8,128)(2,1)S(1)}, u32[]{:S(2)}, u32[]{:S(2)}) collective-permute-start(bf16[256,1,128]{2,0,1:T(8,128)(2,1)S(1)} %collective-permute-done.2), channel_id=1, source_target_pairs={{0,8},{8,16},{16,24},{24,32},{32,40},{40,48},{48,56},{56,64},{64,7... | collective-permute-start | bytes 196616 | tf_op jit(solution)/shard_map/ppermute | solution.py:11
  43.3 11.5 %collective-permute-start.14 = (bf16[256,1,128]{0,2,1:T(8,128)(2,1)S(1)}, bf16[256,1,128]{0,2,1:T(8,128)(2,1)S(1)}, u32[]{:S(2)}, u32[]{:S(2)}) collective-permute-start(bf16[256,1,128]{0,2,1:T(8,128)(2,1)S(1)} %collective-permute-done.13), channel_id=1, source_target_pairs={{0,8},{8,16},{16,24},{24,32},{32,40},{40,48},{48,56},{56,64},{64,7... | collective-permute-start | bytes 196616 | tf_op jit(solution)/shard_map/ppermute | solution.py:11
  46.9 11.5 %collective-permute-start.5 = (bf16[256,1,128]{2,0,1:T(8,128)(2,1)S(1)}, bf16[256,1,128]{2,0,1:T(8,128)(2,1)S(1)}, u32[]{:S(2)}, u32[]{:S(2)}) collective-permute-start(bf16[256,1,128]{2,0,1:T(8,128)(2,1)S(1)} %collective-permute-done.3), channel_id=1, source_target_pairs={{0,8},{8,16},{16,24},{24,32},{32,40},{40,48},{48,56},{56,64},{64,7... | collective-permute-start | bytes 196616 | tf_op jit(solution)/shard_map/ppermute | solution.py:11
  48.9 12.5 %copy-start.19 = (bf16[256,1,128]{2,0,1:T(8,128)(2,1)}, bf16[256,1,128]{2,0,1:T(8,128)(2,1)S(1)}, u32[]{:S(2)}) copy-start(bf16[256,1,128]{2,0,1:T(8,128)(2,1)S(1)} %collective-permute-done.10) | copy-start | bytes 196612
  48.9 11.5 %collective-permute-start.11 = (bf16[256,1,128]{2,0,1:T(8,128)(2,1)S(1)}, bf16[256,1,128]{2,0,1:T(8,128)(2,1)S(1)}, u32[]{:S(2)}, u32[]{:S(2)}) collective-permute-start(bf16[256,1,128]{2,0,1:T(8,128)(2,1)S(1)} %collective-permute-done.10), channel_id=1, source_target_pairs={{0,8},{8,16},{16,24},{24,32},{32,40},{40,48},{48,56},{56,64},{64,7... | collective-permute-start | bytes 196616 | tf_op jit(solution)/shard_map/ppermute | solution.py:11
  52.2 19.7 %collective-permute-start.6 = (bf16[256,1,128]{2,0,1:T(8,128)(2,1)S(1)}, bf16[256,1,128]{2,0,1:T(8,128)(2,1)S(1)}, u32[]{:S(2)}, u32[]{:S(2)}) collective-permute-start(bf16[256,1,128]{2,0,1:T(8,128)(2,1)S(1)} %collective-permute-done.4), channel_id=1, source_target_pairs={{0,8},{8,16},{16,24},{24,32},{32,40},{40,48},{48,56},{56,64},{64,7... | collective-permute-start | bytes 196616 | tf_op jit(solution)/shard_map/ppermute | solution.py:11
  54.1 7.3 %copy-start.25 = (f32[4,256]{1,0:T(4,128)S(1)}, f32[4,256]{1,0:T(4,128)}, u32[]{:S(2)}) copy-start(f32[4,256]{1,0:T(4,128)} %fusion.82) | copy-start | bytes 12292
  54.1 7.3 %copy-start.3 = (f32[1,4,256,256]{2,3,1,0:T(8,128)S(1)}, f32[1,4,256,256]{2,3,1,0:T(8,128)}, u32[]{:S(2)}) copy-start(f32[1,4,256,256]{2,3,1,0:T(8,128)} %copy-done.2) | copy-start | bytes 3145732
  54.5 19.9 %copy-start.1 = (f32[1,4,256,256]{2,3,1,0:T(8,128)}, f32[1,4,256,256]{2,3,1,0:T(8,128)S(1)}, u32[]{:S(2)}) copy-start(f32[1,4,256,256]{2,3,1,0:T(8,128)S(1)} %get-tuple-element.49) | copy-start | bytes 3145732
  54.5 11.5 %copy-start.15 = (bf16[256,1,128]{2,0,1:T(8,128)(2,1)S(1)}, bf16[256,1,128]{2,0,1:T(8,128)(2,1)}, u32[]{:S(2)}) copy-start(bf16[256,1,128]{2,0,1:T(8,128)(2,1)} %param.16) | copy-start | bytes 196612
  54.8 13.4 %collective-permute-start.15 = (bf16[256,1,128]{0,2,1:T(8,128)(2,1)S(1)}, bf16[256,1,128]{0,2,1:T(8,128)(2,1)S(1)}, u32[]{:S(2)}, u32[]{:S(2)}) collective-permute-start(bf16[256,1,128]{0,2,1:T(8,128)(2,1)S(1)} %collective-permute-done.14), channel_id=1, source_target_pairs={{0,8},{8,16},{16,24},{24,32},{32,40},{40,48},{48,56},{56,64},{64,7... | collective-permute-start | bytes 196616 | tf_op jit(solution)/shard_map/ppermute | solution.py:11
  58.4 21.2 %collective-permute-start.7 = (bf16[256,1,128]{2,0,1:T(8,128)(2,1)S(1)}, bf16[256,1,128]{2,0,1:T(8,128)(2,1)}, u32[]{:S(2)}, u32[]{:S(2)}) collective-permute-start(bf16[256,1,128]{2,0,1:T(8,128)(2,1)S(1)} %collective-permute-done.5), channel_id=1, source_target_pairs={{0,8},{8,16},{16,24},{24,32},{32,40},{40,48},{48,56},{56,64},{64,7... | collective-permute-start | bytes 196616 | tf_op jit(solution)/shard_map/ppermute | solution.py:11
  60.4 6.0 %copy-start.22 = (bf16[256,1,128]{2,0,1:T(8,128)(2,1)}, bf16[256,1,128]{2,0,1:T(8,128)(2,1)S(1)}, u32[]{:S(2)}) copy-start(bf16[256,1,128]{2,0,1:T(8,128)(2,1)S(1)} %collective-permute-done.11) | copy-start | bytes 196612
  60.7 14.0 %copy-start.4 = (f32[1,4,256,256]{2,3,1,0:T(8,128)}, f32[1,4,256,256]{2,3,1,0:T(8,128)S(1)}, u32[]{:S(2)}) copy-start(f32[1,4,256,256]{2,3,1,0:T(8,128)S(1)} %get-tuple-element.47) | copy-start | bytes 3145732
  62.4 96.1 %collective-permute-start.21 = (bf16[256,1,128]{2,0,1:T(8,128)(2,1)}, bf16[256,1,128]{2,0,1:T(8,128)(2,1)}, u32[]{:S(2)}, u32[]{:S(2)}) collective-permute-start(bf16[256,1,128]{2,0,1:T(8,128)(2,1)} %fusion.69), channel_id=1, source_target_pairs={{0,8},{8,16},{16,24},{24,32},{32,40},{40,48},{48,56},{56,64},{64,7... | collective-permute-start | bytes 196616 | tf_op jit(solution)/shard_map/ppermute | solution.py:11
  68.8 3.4 %copy-start.14 = (bf16[4,256,256]{1,2,0:T(8,128)(2,1)}, bf16[4,256,256]{1,2,0:T(8,128)(2,1)S(1)}, u32[]{:S(2)}) copy-start(bf16[4,256,256]{1,2,0:T(8,128)(2,1)S(1)} %fusion.36) | copy-start | bytes 1572868
  69.7 91.8 %collective-permute-start.16 = (bf16[256,1,128]{2,0,1:T(8,128)(2,1)}, bf16[256,1,128]{2,0,1:T(8,128)(2,1)}, u32[]{:S(2)}, u32[]{:S(2)}) collective-permute-start(bf16[256,1,128]{2,0,1:T(8,128)(2,1)} %fusion.70), channel_id=1, source_target_pairs={{0,8},{8,16},{16,24},{24,32},{32,40},{40,48},{48,56},{56,64},{64,7... | collective-permute-start | bytes 196616 | tf_op jit(solution)/shard_map/ppermute | solution.py:11
  74.3 5.0 %copy-start.9 = (bf16[4,256,256]{1,2,0:T(8,128)(2,1)}, bf16[4,256,256]{1,2,0:T(8,128)(2,1)S(1)}, u32[]{:S(2)}) copy-start(bf16[4,256,256]{1,2,0:T(8,128)(2,1)S(1)} %fusion.38) | copy-start | bytes 1572868
  147.1 6.1 %copy-start.16 = (bf16[256,1,128]{2,0,1:T(8,128)(2,1)S(1)}, bf16[256,1,128]{2,0,1:T(8,128)(2,1)}, u32[]{:S(2)}) copy-start(bf16[256,1,128]{2,0,1:T(8,128)(2,1)} %param.15) | copy-start | bytes 196612
  152.8 3.8 %copy-start.5 = (f32[1,4,256,256]{2,3,1,0:T(8,128)S(1)}, f32[1,4,256,256]{2,3,1,0:T(8,128)}, u32[]{:S(2)}) copy-start(f32[1,4,256,256]{2,3,1,0:T(8,128)} %copy-done.4) | copy-start | bytes 3145732
  152.9 4.2 %copy-start.13 = (bf16[4,256,256]{1,2,0:T(8,128)(2,1)S(1)}, bf16[4,256,256]{1,2,0:T(8,128)(2,1)}, u32[]{:S(2)}) copy-start(bf16[4,256,256]{1,2,0:T(8,128)(2,1)} %fusion.37) | copy-start | bytes 1572868
  152.9 4.5 %copy-start.10 = (bf16[4,256,256]{1,2,0:T(8,128)(2,1)S(1)}, bf16[4,256,256]{1,2,0:T(8,128)(2,1)}, u32[]{:S(2)}) copy-start(bf16[4,256,256]{1,2,0:T(8,128)(2,1)} %copy-done.9) | copy-start | bytes 1572868
  152.9 4.5 %copy-start.18 = (bf16[256,1,128]{2,0,1:T(8,128)(2,1)S(1)}, bf16[256,1,128]{2,0,1:T(8,128)(2,1)}, u32[]{:S(2)}) copy-start(bf16[256,1,128]{2,0,1:T(8,128)(2,1)} %copy-done.17) | copy-start | bytes 196612
  153.2 4.6 %copy-start.20 = (bf16[256,1,128]{2,0,1:T(8,128)(2,1)S(1)}, bf16[256,1,128]{2,0,1:T(8,128)(2,1)}, u32[]{:S(2)}) copy-start(bf16[256,1,128]{2,0,1:T(8,128)(2,1)} %copy-done.19) | copy-start | bytes 196612
  157.4 43.0 %copy-start.23 = (bf16[256,1,128]{2,0,1:T(8,128)(2,1)S(1)}, bf16[256,1,128]{2,0,1:T(8,128)(2,1)}, u32[]{:S(2)}) copy-start(bf16[256,1,128]{2,0,1:T(8,128)(2,1)} %copy-done.22) | copy-start | bytes 196612
  159.6 5.3 %collective-permute-start.22 = (bf16[256,1,128]{2,0,1:T(8,128)(2,1)S(1)}, bf16[256,1,128]{2,0,1:T(8,128)(2,1)S(1)}, u32[]{:S(2)}, u32[]{:S(2)}) collective-permute-start(bf16[256,1,128]{2,0,1:T(8,128)(2,1)S(1)} %add_convert_fusion.3), channel_id=1, source_target_pairs={{0,8},{8,16},{16,24},{24,32},{32,40},{40,48},{48,56},{56,64},{64,7... | collective-permute-start | bytes 196616 | tf_op jit(solution)/shard_map/ppermute | solution.py:11
  162.7 4.9 %collective-permute-start.17 = (bf16[256,1,128]{2,0,1:T(8,128)(2,1)S(1)}, bf16[256,1,128]{2,0,1:T(8,128)(2,1)S(1)}, u32[]{:S(2)}, u32[]{:S(2)}) collective-permute-start(bf16[256,1,128]{2,0,1:T(8,128)(2,1)S(1)} %add_convert_fusion.7), channel_id=1, source_target_pairs={{0,8},{8,16},{16,24},{24,32},{32,40},{40,48},{48,56},{56,64},{64,7... | collective-permute-start | bytes 196616 | tf_op jit(solution)/shard_map/ppermute | solution.py:11
  164.9 12.1 %collective-permute-start.23 = (bf16[256,1,128]{2,0,1:T(8,128)(2,1)S(1)}, bf16[256,1,128]{2,0,1:T(8,128)(2,1)S(1)}, u32[]{:S(2)}, u32[]{:S(2)}) collective-permute-start(bf16[256,1,128]{2,0,1:T(8,128)(2,1)S(1)} %add_convert_fusion.2), channel_id=1, source_target_pairs={{0,8},{8,16},{16,24},{24,32},{32,40},{40,48},{48,56},{56,64},{64,7... | collective-permute-start | bytes 196616 | tf_op jit(solution)/shard_map/ppermute | solution.py:11
  167.7 14.0 %collective-permute-start.18 = (bf16[256,1,128]{2,0,1:T(8,128)(2,1)S(1)}, bf16[256,1,128]{2,0,1:T(8,128)(2,1)S(1)}, u32[]{:S(2)}, u32[]{:S(2)}) collective-permute-start(bf16[256,1,128]{2,0,1:T(8,128)(2,1)S(1)} %add_convert_fusion.6), channel_id=1, source_target_pairs={{0,8},{8,16},{16,24},{24,32},{32,40},{40,48},{48,56},{56,64},{64,7... | collective-permute-start | bytes 196616 | tf_op jit(solution)/shard_map/ppermute | solution.py:11
  177.1 14.3 %collective-permute-start.24 = (bf16[256,1,128]{2,0,1:T(8,128)(2,1)S(1)}, bf16[256,1,128]{2,0,1:T(8,128)(2,1)S(1)}, u32[]{:S(2)}, u32[]{:S(2)}) collective-permute-start(bf16[256,1,128]{2,0,1:T(8,128)(2,1)S(1)} %add_convert_fusion.1), channel_id=1, source_target_pairs={{0,8},{8,16},{16,24},{24,32},{32,40},{40,48},{48,56},{56,64},{64,7... | collective-permute-start | bytes 196616 | tf_op jit(solution)/shard_map/ppermute | solution.py:11
  181.7 16.7 %collective-permute-start.19 = (bf16[256,1,128]{2,0,1:T(8,128)(2,1)S(1)}, bf16[256,1,128]{2,0,1:T(8,128)(2,1)S(1)}, u32[]{:S(2)}, u32[]{:S(2)}) collective-permute-start(bf16[256,1,128]{2,0,1:T(8,128)(2,1)S(1)} %add_convert_fusion.5), channel_id=1, source_target_pairs={{0,8},{8,16},{16,24},{24,32},{32,40},{40,48},{48,56},{56,64},{64,7... | collective-permute-start | bytes 196616 | tf_op jit(solution)/shard_map/ppermute | solution.py:11
  191.4 11.9 %collective-permute-start.25 = (bf16[256,1,128]{2,0,1:T(8,128)(2,1)S(1)}, bf16[256,1,128]{2,0,1:T(8,128)(2,1)S(1)}, u32[]{:S(2)}, u32[]{:S(2)}) collective-permute-start(bf16[256,1,128]{2,0,1:T(8,128)(2,1)S(1)} %add_convert_fusion), channel_id=1, source_target_pairs={{0,480},{8,488},{16,496},{24,504},{32,0},{40,8},{48,16},{56,24},{6... | collective-permute-start | bytes 196616 | tf_op jit(solution)/shard_map/ppermute | solution.py:11
  198.5 14.4 %collective-permute-start.20 = (bf16[256,1,128]{2,0,1:T(8,128)(2,1)S(1)}, bf16[256,1,128]{2,0,1:T(8,128)(2,1)S(1)}, u32[]{:S(2)}, u32[]{:S(2)}) collective-permute-start(bf16[256,1,128]{2,0,1:T(8,128)(2,1)S(1)} %add_convert_fusion.4), channel_id=1, source_target_pairs={{0,480},{8,488},{16,496},{24,504},{32,0},{40,8},{48,16},{56,24},{6... | collective-permute-start | bytes 196616 | tf_op jit(solution)/shard_map/ppermute | solution.py:11
  (6 other events, 15.4 us)
Sparse Core Ops, SparseCore 0:
  20.5 126.5 all-gather.1
  153.0 144.5 reduce-scatter.1
where the time goes:
time: 307 us; the launch traced here: 306 us
  waiting for transfers between devices  181 us (59%)
  starting transfers between devices  72.9 us (24%)
  matrix products  29.4 us (10%)
  between operations  15.8 us (5%)
  local copies, waits for them, and re-layouts  3.44 us (1%)
    reduce_scatter x1, waiting for transfers between devices, local(): lax.psum_scatter(partial_terms.astype(jnp.bfloat16), 'head', scatter_dime...  84.7 us
    ppermute x26, starting transfers between devices, from_behind(): lax.ppermute(x, axis, [(i, (i + by) % devices) for i in range(devices)])  72.8 us
    all_gather x1, waiting for transfers between devices, local(): weight_piece = lax.all_gather(out_weight, 'ctx', axis=2, tiled=True)  67.5 us
    ppermute x26, waiting for transfers between devices, from_behind(): lax.ppermute(x, axis, [(i, (i + by) % devices) for i in range(devices)])  29 us
  transfers between devices with their start and end apart: 28, of which 8 were waited for; matrix products, arithmetic and copies ran while one was open for 11% of the time, Pallas kernels for 0%

commit v1 on v0

v1 whole, which is shorter than its diff:
```python
import functools
import math

import jax
import jax.numpy as jnp
from jax import lax
from jax.experimental import pallas as pl
from jax.experimental.pallas import tpu as pltpu
from jax.sharding import PartitionSpec as P

Z, Y, X = 8, 4, 4
ROWS, HEADS, DIM = 256, 4, 128
QROWS = ROWS * HEADS
HOPS = 4
CHUNKS, CHUNK = 4, 256
SCALE = DIM**-0.5
SCALE2 = SCALE * math.log2(math.e)
NEG = -1e30
MESH = pl.DeviceIdType.MESH
F32, BF16 = jnp.float32, jnp.bfloat16


def dot(a, b, dims):
    return lax.dot_general(a, b, (dims, ((), ())), preferred_element_type=F32)


def nt(a, b):
    return dot(a, b, ((1,), (1,)))


def nn(a, b):
    return dot(a, b, ((1,), (0,)))


class Place:
    def __init__(self, ctx, head):
        self.ctx, self.head = ctx, head
        self.z, self.y, self.core = ctx // 8, (ctx // 2) % 4, ctx % 2
        self.x, self.half = head // 2, head % 2

    def at(self, z=None, y=None, core=None, x=None, half=None):
        z = self.z if z is None else z
        y = self.y if y is None else y
        core = self.core if core is None else core
        x = self.x if x is None else x
        half = self.half if half is None else half
        return ((z * Y + y) * 2 + core, x * 2 + half)

    def sibling(self):
        return self.at(core=1 - self.core)

    def along_x(self, by):
        return self.at(x=(self.x + by + X) % X)

    def along_y(self, by):
        return self.at(y=(self.y + by + Y) % Y)

    def quad(self, by):
        return self.at(z=self.z // 4 * 4 + (self.z + by + 4) % 4)

    def other_half(self):
        return self.at(half=1 - self.half)

    def chip(self, by):
        return ((self.ctx + 2 * by + 64) % 64, self.head)

    def turned(self, by):
        return ((self.head + by) % Z * 8 + self.ctx % 8, self.z)

    def turned_from(self, by):
        return (self.head * 8 + self.ctx % 8, (self.z - by + Z) % Z)


def kernel(
    order_ref, qb_ref, kb_ref, vb_ref, w_ref, qa_ref, ka_ref, va_ref, ga_ref,
    out_ref, dq_ref, dk_ref, dv_ref,
    kv_b, kv_a, wt, att, s_buf, dp_buf, rows_buf, acc, dqt, m_buf, l_buf, d_buf,
    dkv, gsend, grecv, send_sem, recv_sem,
):
    me = Place(lax.axis_index("ctx"), lax.axis_index("head"))
    core = me.core
    own_block = order_ref[0]

    sources = [me.sibling(), me.other_half()]
    sources += [me.along_x(by) for by in (1, 2, 3)]
    sources += [me.along_y(by) for by in (1, 2, 3)]
    sources += [me.quad(by) for by in (1, 2, 3)]
    sources += [me.chip(by) for by in (1, 2, -1, -2)]
    sources += [me.turned_from(1), me.turned_from(5)]
    barrier = pltpu.get_barrier_semaphore()
    for source in sources:
        pl.semaphore_signal(barrier, inc=1, device_id=source, device_id_type=MESH)

    started = []

    def send(src, dst, target):
        at = len(started)
        copy = pltpu.make_async_remote_copy(
            src_ref=src, dst_ref=dst, send_sem=send_sem.at[at], recv_sem=recv_sem.at[at],
            device_id=target, device_id_type=MESH,
        )
        copy.start()
        started.append(copy)
        return copy

    kv_b[0, 0] = kb_ref[...]
    kv_b[0, 1] = vb_ref[...]
    kv_a[0, 0] = ka_ref[...]
    kv_a[0, 1] = va_ref[...]

    def masked(s, hop, c):
        if hop not in (0, HOPS):
            return s
        key = lax.broadcasted_iota(jnp.int32, s.shape, 0)
        token = c * (CHUNK // HEADS) + lax.broadcasted_iota(jnp.int32, s.shape, 1) // HEADS
        return jnp.where(token >= key if hop == 0 else token < key, s, NEG)

    def stats(s, hop, c):
        top = jnp.max(s, axis=0, keepdims=True)
        if hop == 0:
            return top, top * SCALE2, None
        seen = own_block >= hop
        before = m_buf[c]
        top = jnp.maximum(before, jnp.where(seen, top, NEG))
        return top, jnp.where(seen, top * SCALE2, -NEG), jnp.exp2((before - top) * SCALE2)

    def forward_b(hop):
        vt = kv_b[hop, 1].T

        def step(c, _):
            s = masked(nt(kv_b[hop, 0], qb_ref[pl.ds(c * CHUNK, CHUNK), :]), hop, c)
            top, minus, factor = stats(s, hop, c)
            p = jnp.exp2(s * SCALE2 - minus)
            total = jnp.sum(p, axis=0, keepdims=True)
            part = nn(vt, p.astype(BF16))
            m_buf[c] = top
            if hop == 0:
                l_buf[c] = total
                acc[c] = part
            else:
                l_buf[c] = l_buf[c] * factor + total
                acc[c] = acc[c] * factor + part
            return 0

        lax.fori_loop(0, CHUNKS, step, 0)

    def forward_a(hop):
        def step(c, _):
            s = masked(nt(kv_a[hop, 0], qa_ref[pl.ds(c * CHUNK, CHUNK), :]), hop, c)
            s_buf[hop, c] = s
            top, minus, factor = stats(s, hop, c)
            p = jnp.exp2(s * SCALE2 - minus)
            total = jnp.sum(p, axis=0, keepdims=True)
            dp = nt(kv_a[hop, 1], ga_ref[pl.ds(c * CHUNK, CHUNK), :])
            dp_buf[hop, c] = dp
            part = jnp.sum(p * dp, axis=0, keepdims=True)
            m_buf[c] = top
            if hop == 0:
                l_buf[c] = total
                d_buf[c] = part
            else:
                l_buf[c] = l_buf[c] * factor + total
                d_buf[c] = d_buf[c] * factor + part
            return 0

        lax.fori_loop(0, CHUNKS, step, 0)

    def backward_a(hop):
        kt = kv_a[hop, 0].T
        dkv[...] = jnp.zeros_like(dkv)

        def step(c, _):
            part = pl.ds(c * CHUNK, CHUNK)
            log_total = l_buf[c]
            if hop:
                log_total = jnp.where(own_block >= hop, log_total, -NEG)
            probs = jnp.exp2(s_buf[hop, c] * SCALE2 - log_total)
            low = probs.astype(BF16)
            ds = (probs * (dp_buf[hop, c] - d_buf[c])).astype(BF16)
            dkv[0] += nn(ds, qa_ref[part, :])
            dkv[1] += nn(low, ga_ref[part, :])
            if hop == 1:
                dqt[c] = nn(kt, ds)
            else:
                dqt[c] += nn(kt, ds)
            return 0

        lax.fori_loop(0, CHUNKS, step, 0)

    forward_b(0)
    pl.semaphore_wait(barrier, len(sources))

    def halo_first(kv):
        return [send(kv.at[0], kv.at[2 * by], me.chip(by)) for by in (1, 2)]

    halo_b = halo_first(kv_b)
    turn = [
        send(w_ref, wt.at[core, me.y, (me.head + 1) % 4, (me.head + 1) % Z // 4], me.turned(by))
        for by in (1, 5)
    ]
    halo_a = halo_first(kv_a)

    def halo_rest(kv, halo):
        halo[0].wait_recv()
        first = send(kv.at[2 * core], kv.at[1], me.sibling())
        halo[1].wait_recv()
        second = send(kv.at[2 + 2 * core], kv.at[3], me.sibling())
        return first, second

    rest_b = halo_rest(kv_b, halo_b)
    forward_b(2)
    forward_b(4)
    rest_b[0].wait_recv()
    forward_b(1)
    rest_b[1].wait_recv()
    forward_b(3)

    def finish_b(c, _):
        rows_buf[pl.ds(c * CHUNK, CHUNK), :] = (acc[c] / l_buf[c]).T
        return 0

    lax.fori_loop(0, CHUNKS, finish_b, 0)
    across, beside = [], []
    for h in range(HEADS):
        att[me.head, h] = rows_buf[pl.ds(h, ROWS, stride=HEADS), :].astype(BF16)
        mine = att.at[me.head, h]
        across.append(send(mine, mine, me.other_half()))
        for by in (1, 2, 3):
            beside.append(send(mine, mine, me.along_x(by)))

    own = me.z % 4
    in_quad, in_row, in_chip = [], [], []
    for copy in turn:
        copy.wait_recv()
    pair = wt.at[core, me.y, own]
    for by in (1, 2, 3):
        in_quad.append(send(pair, pair, me.quad(by)))

    def spread(q):
        pair = wt.at[core, me.y, q]
        got = [send(pair, pair, me.along_y(by)) for by in (1, 3, 2)]
        in_chip.append(send(pair, pair, me.sibling()))
        return [(copy, by, q) for copy, by in zip(got, (1, 3, 2))]

    in_row += spread(own)

    rest_a = halo_rest(kv_a, halo_a)
    forward_a(0)
    forward_a(2)
    for by in (1, 2, 3):
        in_quad[by - 1].wait_recv()
        in_row += spread((me.z + 4 - by) % 4)
        if by == 1:
            forward_a(4)
        elif by == 2:
            rest_a[0].wait_recv()
            forward_a(1)
    rest_a[1].wait_recv()
    forward_a(3)

    def finish_stats(c, _):
        d_buf[c] = d_buf[c] / l_buf[c]
        l_buf[c] = m_buf[c] * SCALE2 + jnp.log2(l_buf[c])
        return 0

    lax.fori_loop(0, CHUNKS, finish_stats, 0)

    def to_sibling(copy, by, q):
        copy.wait_recv()
        pair = wt.at[core, (me.y - by + Y) % Y, q]
        in_chip.append(send(pair, pair, me.sibling()))

    passed = []

    def to_row(h):
        across[h].wait_recv()
        theirs = att.at[me.head + 1 - 2 * me.half, h]
        for by in (1, 2, 3):
            passed.append(send(theirs, theirs, me.along_x(by)))

    def to_send(at):
        gsend[at, 0] = (dkv[0] * SCALE).astype(BF16)
        gsend[at, 1] = dkv[1].astype(BF16)

    def add(at, weight):
        dkv[0] += grecv[at, 0].astype(F32) * (weight / SCALE)
        dkv[1] += grecv[at, 1].astype(F32) * weight

    backward_a(1)
    to_send(0)
    grad_1 = send(gsend.at[0], grecv.at[0], me.sibling())
    for item in in_row[:3]:
        to_sibling(*item)
    backward_a(3)
    to_send(1)
    grad_3 = send(gsend.at[1], grecv.at[1], me.sibling())
    for item in in_row[3:6]:
        to_sibling(*item)
    backward_a(2)
    grad_1.wait_recv()
    grad_3.wait_recv()
    add(1 - core, 1.0)
    to_send(2)
    grad_2 = send(gsend.at[2], grecv.at[2], me.chip(-1))
    backward_a(4)
    add(1, core.astype(F32))
    to_send(3)
    grad_4 = send(gsend.at[3], grecv.at[3], me.chip(-2))
    to_row(0)
    for item in in_row[6:9]:
        to_sibling(*item)
    backward_a(0)
    to_row(1)
    for item in in_row[9:]:
        to_sibling(*item)

    def finish_dq(c, _):
        dq_ref[pl.ds(c * CHUNK, CHUNK), :] = (dqt[c] * SCALE).T.astype(BF16)
        return 0

    lax.fori_loop(0, CHUNKS, finish_dq, 0)
    add(0, (1 - core).astype(F32))
    to_row(2)
    to_row(3)
    grad_2.wait_recv()
    grad_4.wait_recv()
    add(2, 1.0)
    add(3, 1.0)
    dk_ref[...] = (dkv[0] * SCALE).astype(BF16)
    dv_ref[...] = dkv[1].astype(BF16)

    for copy in beside + in_chip + passed:
        copy.wait_recv()
    total = None
    for q in range(4):
        for hi in range(2):
            head = (hi * 4 + q - 1) % Z
            rhs = jnp.concatenate(
                [
                    jnp.concatenate([wt[k, y, q, hi, h] for y in range(Y) for k in range(2)], axis=0)
                    for h in range(HEADS)
                ],
                axis=1,
            )
            lhs = jnp.concatenate([att[head, h] for h in range(HEADS)], axis=1)
            term = nt(lhs, rhs)
            total = term if total is None else total + term
    out_ref[...] = total.astype(BF16)
    for copy in started:
        copy.wait_send()


SENDS = 100


def local(block_order, query_b, key_b, value_b, out_weight, query_a, key_a, value_a, grad_a):
    flat_q = lambda a: a.reshape(QROWS, DIM)
    flat_k = lambda a: a.reshape(ROWS, DIM)
    vmem = pl.BlockSpec(memory_space=pltpu.VMEM)
    out, dq, dk, dv = pl.pallas_call(
        kernel,
        out_shape=(
            jax.ShapeDtypeStruct((ROWS, 512), BF16),
            jax.ShapeDtypeStruct((QROWS, DIM), BF16),
            jax.ShapeDtypeStruct((ROWS, DIM), BF16),
            jax.ShapeDtypeStruct((ROWS, DIM), BF16),
        ),
        in_specs=[pl.BlockSpec(memory_space=pltpu.SMEM)] + [vmem] * 8,
        out_specs=(vmem,) * 4,
        scratch_shapes=[
            pltpu.VMEM((5, 2, ROWS, DIM), BF16),
            pltpu.VMEM((5, 2, ROWS, DIM), BF16),
            pltpu.VMEM((2, Y, 4, 2, HEADS, 64, DIM), BF16),
            pltpu.VMEM((8, HEADS, ROWS, DIM), BF16),
            pltpu.VMEM((5, CHUNKS, ROWS, CHUNK), F32),
            pltpu.VMEM((5, CHUNKS, ROWS, CHUNK), F32),
            pltpu.VMEM((QROWS, DIM), F32),
            pltpu.VMEM((CHUNKS, DIM, CHUNK), F32),
            pltpu.VMEM((CHUNKS, DIM, CHUNK), F32),
            pltpu.VMEM((CHUNKS, 1, CHUNK), F32),
            pltpu.VMEM((CHUNKS, 1, CHUNK), F32),
            pltpu.VMEM((CHUNKS, 1, CHUNK), F32),
            pltpu.VMEM((2, ROWS, DIM), F32),
            pltpu.VMEM((4, 2, ROWS, DIM), BF16),
            pltpu.VMEM((4, 2, ROWS, DIM), BF16),
            pltpu.SemaphoreType.DMA((SENDS,)),
            pltpu.SemaphoreType.DMA((SENDS,)),
        ],
        compiler_params=pltpu.CompilerParams(
            collective_id=0, has_side_effects=True, vmem_limit_bytes=48 * 2**20
        ),
        name="attention",
    )(
        block_order, flat_q(query_b), flat_k(key_b), flat_k(value_b),
        jnp.transpose(out_weight, (0, 2, 1)),
        flat_q(query_a), flat_k(key_a), flat_k(value_a), flat_q(grad_a),
    )
    flat = (ROWS, 1, DIM)
    return out, dq.reshape(ROWS, HEADS, DIM), dk.reshape(flat), dv.reshape(flat)


def solution(mesh):
    heads = P("ctx", "head", None)
    return jax.shard_map(
        local,
        mesh=mesh,
        in_specs=(P("ctx"), heads, heads, heads, P("head", None, "ctx"), heads, heads, heads, heads),
        out_specs=(P("ctx", "head"), heads, heads, heads),
        check_vma=False,
    )
```

time: 307 us -> 109 us (0.36)
  waiting for transfers between devices: 181 us -> 0 us
  Pallas kernels: 0 us -> 98 us
  starting transfers between devices: 72.9 us -> 0 us
  matrix products: 29.4 us -> 0 us
  between operations: 15.8 us -> 1.3 us
  local copies, waits for them, and re-layouts: 3.44 us -> 9.7 us
    pallas_call x0 -> x1, Pallas kernels: none -> 98 us  [local(): pl.pallas_call(kernel, out_shape=(jax.ShapeDtypeStruct((ROWS, 512), BF16)...]
    reduce_scatter x1 -> x0, waiting for transfers between devices: 84.7 us -> none  [local(): lax.psum_scatter(partial_terms.astype(jnp.bfloat16), 'head', scatter_dime...]
    ppermute x26 -> x0, starting transfers between devices: 72.8 us -> none  [from_behind(): lax.ppermute(x, axis, [(i, (i + by) % devices) for i in range(devices)])]
    all_gather x1 -> x0, waiting for transfers between devices: 67.5 us -> none  [local(): weight_piece = lax.all_gather(out_weight, 'ctx', axis=2, tiled=True)]
    dot_general x40 -> x0, matrix products: 29.4 us -> none  [the longest x1 5.7 us: local(): jnp.einsum('kgrd,kgdn->rn', attended, weight4, preferred_element_type=jnp...]
    ppermute x26 -> x0, waiting for transfers between devices: 29 us -> none  [from_behind(): lax.ppermute(x, axis, [(i, (i + by) % devices) for i in range(devices)])]
    unnamed x57 -> x20, local copies, waits for them, and re-layouts: 3.44 us -> 9.7 us
  transfers between devices with their start and end apart: 28 -> 0, of which waited for: 8 -> 0; matrix products, arithmetic and copies ran while one was open for 11% -> 0% of each run, Pallas kernels for 0% -> 0%
where the time goes in v1:
time: 109 us
  Pallas kernels  98 us (90%)
  local copies, waits for them, and re-layouts  9.7 us (9%)
  between operations  1.3 us (1%)
    pallas_call x1, Pallas kernels, local(): pl.pallas_call(kernel, out_shape=(jax.ShapeDtypeStruct((ROWS, 512), BF16)...  98 us
    unnamed x20, local copies, waits for them, and re-layouts  9.7 us

profile of v1, /device:TPU:1, one launch (start us, length us, event | category | flops | bytes accessed | tf_op | source)
XLA Modules:
  0.0 109.0 jit_solution(17915954116458936651)
XLA Ops:
  1.3 0.0 copy-start
  1.3 0.9 copy-done
  2.2 0.0 copy-start.1
  2.2 0.9 copy-done.1
  3.2 0.0 copy-start.2
  3.2 0.9 copy-done.2
  4.1 0.0 copy-start.3
  4.1 0.8 copy-done.3
  5.0 0.0 copy-start.4
  5.0 0.8 copy-done.4
  5.8 0.0 copy-start.5
  5.8 0.8 copy-done.5
  6.7 0.0 copy-start.6
  6.7 0.8 copy-done.6
  7.5 0.0 copy-start.7
  7.5 0.8 copy-done.7
  8.3 98.0 %attention.1 = (bf16[256,512]{1,0:T(8,128)(2,1)S(1)}, bf16[1024,128]{1,0:T(8,128)(2,1)S(1)}, bf16[256,128]{1,0:T(8,128)(2,1)S(1)}, bf16[256,128]{1,0:T(8,128)(2,1)S(1)}) custom-call(s32[1]{0:T(128)S(6)} %copy.17.order_ref, bf16[1024,128]{1,0:T(8,128)(2,1)S(1)} %bitcast.12, bf16[256,128]{1,0:T(8,128)(2,1)S(1)} %bitcast.15, bf16[256,128]{1,0:T(8,128)(2,1)S(1)} %bitcast.16, ...), custom_call_target="tpu_custom_call" | custom-call | tf_op jit(solution)/shard_map/attention/pallas_call | solution.py:360
  106.4 0.7 copy.18
  107.1 0.7 copy.19
  107.8 0.6 copy.20
  108.4 0.6 copy.21
Async XLA Ops:
  1.3 1.0 copy-start
  2.2 0.9 copy-start.1
  3.2 0.9 copy-start.2
  4.1 0.8 copy-start.3
  5.0 0.8 copy-start.4
  5.8 0.8 copy-start.5
  6.7 0.8 copy-start.6
  7.5 0.8 copy-start.7

commit v2 on v1

--- a/solution.py
+++ b/solution.py
@@ -72,24 +72,35 @@
 
 
 def kernel(
-    order_ref, qb_ref, kb_ref, vb_ref, w_ref, qa_ref, ka_ref, va_ref, ga_ref,
+    order_ref, qb_hbm, kb_hbm, vb_hbm, w_ref, qa_hbm, ka_hbm, va_hbm, ga_hbm,
     out_ref, dq_ref, dk_ref, dv_ref,
-    kv_b, kv_a, wt, att, s_buf, dp_buf, rows_buf, acc, dqt, m_buf, l_buf, d_buf,
-    dkv, gsend, grecv, send_sem, recv_sem,
+    qb_ref, qa_ref, ga_ref,
+    kv_b, kv_a, wt, att, s_buf, dp_buf, rows_buf, acc, dqt, m_buf, l_buf, d_buf, mb_buf, lb_buf, vt_buf, sa_buf,
+    dkv, gsend, grecv, send_sem, recv_sem, load_sem,
 ):
     me = Place(lax.axis_index("ctx"), lax.axis_index("head"))
     core = me.core
     own_block = order_ref[0]
 
-    sources = [me.sibling(), me.other_half()]
+    sources = [me.other_half(), me.turned_from(1), me.turned_from(5)]
+    sources += [me.chip(by) for by in (1, 2, -1, -2)]
     sources += [me.along_x(by) for by in (1, 2, 3)]
     sources += [me.along_y(by) for by in (1, 2, 3)]
     sources += [me.quad(by) for by in (1, 2, 3)]
-    sources += [me.chip(by) for by in (1, 2, -1, -2)]
-    sources += [me.turned_from(1), me.turned_from(5)]
+    sources += [me.sibling()]
     barrier = pltpu.get_barrier_semaphore()
     for source in sources:
         pl.semaphore_signal(barrier, inc=1, device_id=source, device_id_type=MESH)
+
+    loads = [
+        (kb_hbm, kv_b.at[0, 0]), (qb_hbm, qb_ref), (vb_hbm, kv_b.at[0, 1]),
+        (ka_hbm, kv_a.at[0, 0]), (qa_hbm, qa_ref), (va_hbm, kv_a.at[0, 1]), (ga_hbm, ga_ref),
+    ]
+    loads = [
+        pltpu.make_async_copy(src, dst, load_sem.at[at]) for at, (src, dst) in enumerate(loads)
+    ]
+    for load in loads:
+        load.start()
 
     started = []
 
@@ -103,11 +114,6 @@
         started.append(copy)
         return copy
 
-    kv_b[0, 0] = kb_ref[...]
-    kv_b[0, 1] = vb_ref[...]
-    kv_a[0, 0] = ka_ref[...]
-    kv_a[0, 1] = va_ref[...]
-
     def masked(s, hop, c):
         if hop not in (0, HOPS):
             return s
@@ -124,30 +130,54 @@
         top = jnp.maximum(before, jnp.where(seen, top, NEG))
         return top, jnp.where(seen, top * SCALE2, -NEG), jnp.exp2((before - top) * SCALE2)
 
-    def forward_b(hop):
-        vt = kv_b[hop, 1].T
+    def scores(kv, q_ref, hop, c):
+        return masked(nt(kv[hop, 0], q_ref[pl.ds(c * CHUNK, CHUNK), :]), hop, c)
+
+    def own_b():
+        vt = kv_b[0, 1].T
 
         def step(c, _):
-            s = masked(nt(kv_b[hop, 0], qb_ref[pl.ds(c * CHUNK, CHUNK), :]), hop, c)
-            top, minus, factor = stats(s, hop, c)
-            p = jnp.exp2(s * SCALE2 - minus)
-            total = jnp.sum(p, axis=0, keepdims=True)
-            part = nn(vt, p.astype(BF16))
-            m_buf[c] = top
-            if hop == 0:
-                l_buf[c] = total
-                acc[c] = part
-            else:
-                l_buf[c] = l_buf[c] * factor + total
-                acc[c] = acc[c] * factor + part
+            s = scores(kv_b, qb_ref, 0, c)
+            top = jnp.max(s, axis=0, keepdims=True)
+            p = jnp.exp2((s - top) * SCALE2)
+            mb_buf[c] = top
+            lb_buf[c] = jnp.sum(p, axis=0, keepdims=True)
+            acc[c] = nn(vt, p.astype(BF16))
             return 0
 
         lax.fori_loop(0, CHUNKS, step, 0)
+
+    def scores_b(hop):
+        def step(c, _):
+            s_buf[hop, c] = scores(kv_b, qb_ref, hop, c)
+            return 0
+
+        lax.fori_loop(0, CHUNKS, step, 0)
+
+    def rest_of_b(c):
+        before = mb_buf[c]
+        top = before
+        for hop in (1, 2, 3, 4):
+            if hop in (1, 3):
+                s_buf[hop, c] = scores(kv_b, qb_ref, hop, c)
+            block_top = jnp.max(s_buf[hop, c], axis=0, keepdims=True)
+            top = jnp.maximum(top, jnp.where(own_block >= hop, block_top, NEG))
+        factor = jnp.exp2((before - top) * SCALE2)
+        total = lb_buf[c] * factor
+        weighted = acc[c] * factor
+        for hop in (1, 2, 3, 4):
+            minus = jnp.where(own_block >= hop, top * SCALE2, -NEG)
+            p = jnp.exp2(s_buf[hop, c] * SCALE2 - minus)
+            total += jnp.sum(p, axis=0, keepdims=True)
+            weighted += nn(vt_buf[hop], p.astype(BF16))
+        rows_buf[...] = (weighted / total).T
+        for h in range(HEADS):
+            att[me.head, c, h] = rows_buf[pl.ds(h, CHUNK // HEADS, stride=HEADS), :].astype(BF16)
 
     def forward_a(hop):
         def step(c, _):
-            s = masked(nt(kv_a[hop, 0], qa_ref[pl.ds(c * CHUNK, CHUNK), :]), hop, c)
-            s_buf[hop, c] = s
+            s = scores(kv_a, qa_ref, hop, c)
+            sa_buf[hop, c] = s
             top, minus, factor = stats(s, hop, c)
             p = jnp.exp2(s * SCALE2 - minus)
             total = jnp.sum(p, axis=0, keepdims=True)
@@ -174,7 +204,7 @@
             log_total = l_buf[c]
             if hop:
                 log_total = jnp.where(own_block >= hop, log_total, -NEG)
-            probs = jnp.exp2(s_buf[hop, c] * SCALE2 - log_total)
+            probs = jnp.exp2(sa_buf[hop, c] * SCALE2 - log_total)
             low = probs.astype(BF16)
             ds = (probs * (dp_buf[hop, c] - d_buf[c])).astype(BF16)
             dkv[0] += nn(ds, qa_ref[part, :])
@@ -187,7 +217,12 @@
 
         lax.fori_loop(0, CHUNKS, step, 0)
 
-    forward_b(0)
+    for load in loads[:3]:
+        load.wait()
+    own_b()
+    for load in loads[3:]:
+        load.wait()
+    forward_a(0)
     pl.semaphore_wait(barrier, len(sources))
 
     def halo_first(kv):
@@ -200,61 +235,69 @@
     ]
     halo_a = halo_first(kv_a)
 
-    def halo_rest(kv, halo):
-        halo[0].wait_recv()
-        first = send(kv.at[2 * core], kv.at[1], me.sibling())
-        halo[1].wait_recv()
-        second = send(kv.at[2 + 2 * core], kv.at[3], me.sibling())
-        return first, second
-
-    rest_b = halo_rest(kv_b, halo_b)
-    forward_b(2)
-    forward_b(4)
-    rest_b[0].wait_recv()
-    forward_b(1)
-    rest_b[1].wait_recv()
-    forward_b(3)
-
-    def finish_b(c, _):
-        rows_buf[pl.ds(c * CHUNK, CHUNK), :] = (acc[c] / l_buf[c]).T
-        return 0
-
-    lax.fori_loop(0, CHUNKS, finish_b, 0)
-    across, beside = [], []
-    for h in range(HEADS):
-        att[me.head, h] = rows_buf[pl.ds(h, ROWS, stride=HEADS), :].astype(BF16)
-        mine = att.at[me.head, h]
-        across.append(send(mine, mine, me.other_half()))
-        for by in (1, 2, 3):
-            beside.append(send(mine, mine, me.along_x(by)))
+    halo_b[0].wait_recv()
+    rest_b = [send(kv_b.at[2 * core], kv_b.at[1], me.sibling())]
+    vt_buf[2] = kv_b[2, 1].T
+    scores_b(2)
+    halo_b[1].wait_recv()
+    rest_b.append(send(kv_b.at[2 + 2 * core], kv_b.at[3], me.sibling()))
+    vt_buf[4] = kv_b[4, 1].T
+    scores_b(4)
+    for copy, hop in zip(rest_b, (1, 3)):
+        copy.wait_recv()
+        vt_buf[hop] = kv_b[hop, 1].T
 
     own = me.z % 4
     in_quad, in_row, in_chip = [], [], []
-    for copy in turn:
-        copy.wait_recv()
-    pair = wt.at[core, me.y, own]
-    for by in (1, 2, 3):
-        in_quad.append(send(pair, pair, me.quad(by)))
 
     def spread(q):
         pair = wt.at[core, me.y, q]
         got = [send(pair, pair, me.along_y(by)) for by in (1, 3, 2)]
         in_chip.append(send(pair, pair, me.sibling()))
-        return [(copy, by, q) for copy, by in zip(got, (1, 3, 2))]
-
-    in_row += spread(own)
-
-    rest_a = halo_rest(kv_a, halo_a)
-    forward_a(0)
+        in_row.append([(copy, by, q) for copy, by in zip(got, (1, 3, 2))])
+
+    def weight_turned():
+        for copy in turn:
+            copy.wait_recv()
+        pair = wt.at[core, me.y, own]
+        for by in (1, 3, 2):
+            in_quad.append(send(pair, pair, me.quad(by)))
+        spread(own)
+
+    def weight_quad(by):
+        in_quad[(1, 3, 2).index(by)].wait_recv()
+        spread((me.z + 4 - by) % 4)
+
+    def weight_row(at):
+        for copy, by, q in in_row[at]:
+            copy.wait_recv()
+            pair = wt.at[core, (me.y - by + Y) % Y, q]
+            in_chip.append(send(pair, pair, me.sibling()))
+
+    across, beside, passed = [], [], []
+    for c in range(CHUNKS):
+        rest_of_b(c)
+        if c == 0:
+            weight_turned()
+        mine = att.at[me.head, c]
+        across.append(send(mine, mine, me.other_half()))
+        for by in (1, 3, 2):
+            beside.append(send(mine, mine, me.along_x(by)))
+
+    def to_row(c):
+        across[c].wait_recv()
+        theirs = att.at[me.head + 1 - 2 * me.half, c]
+        for by in (1, 3, 2):
+            passed.append(send(theirs, theirs, me.along_x(by)))
+
+    halo_a[0].wait_recv()
+    rest_a = [send(kv_a.at[2 * core], kv_a.at[1], me.sibling())]
     forward_a(2)
-    for by in (1, 2, 3):
-        in_quad[by - 1].wait_recv()
-        in_row += spread((me.z + 4 - by) % 4)
-        if by == 1:
-            forward_a(4)
-        elif by == 2:
-            rest_a[0].wait_recv()
-            forward_a(1)
+    halo_a[1].wait_recv()
+    rest_a.append(send(kv_a.at[2 + 2 * core], kv_a.at[3], me.sibling()))
+    forward_a(4)
+    rest_a[0].wait_recv()
+    forward_a(1)
     rest_a[1].wait_recv()
     forward_a(3)
 
@@ -265,19 +308,6 @@
 
     lax.fori_loop(0, CHUNKS, finish_stats, 0)
 
-    def to_sibling(copy, by, q):
-        copy.wait_recv()
-        pair = wt.at[core, (me.y - by + Y) % Y, q]
-        in_chip.append(send(pair, pair, me.sibling()))
-
-    passed = []
-
-    def to_row(h):
-        across[h].wait_recv()
-        theirs = att.at[me.head + 1 - 2 * me.half, h]
-        for by in (1, 2, 3):
-            passed.append(send(theirs, theirs, me.along_x(by)))
-
     def to_send(at):
         gsend[at, 0] = (dkv[0] * SCALE).astype(BF16)
         gsend[at, 1] = dkv[1].astype(BF16)
@@ -286,33 +316,30 @@
         dkv[0] += grecv[at, 0].astype(F32) * (weight / SCALE)
         dkv[1] += grecv[at, 1].astype(F32) * weight
 
+    weight_row(0)
     backward_a(1)
     to_send(0)
     grad_1 = send(gsend.at[0], grecv.at[0], me.sibling())
-    for item in in_row[:3]:
-        to_sibling(*item)
+    weight_quad(1)
     backward_a(3)
     to_send(1)
     grad_3 = send(gsend.at[1], grecv.at[1], me.sibling())
-    for item in in_row[3:6]:
-        to_sibling(*item)
+    weight_quad(3)
+    to_row(0)
     backward_a(2)
     grad_1.wait_recv()
     grad_3.wait_recv()
     add(1 - core, 1.0)
     to_send(2)
     grad_2 = send(gsend.at[2], grecv.at[2], me.chip(-1))
+    weight_quad(2)
+    to_row(1)
     backward_a(4)
     add(1, core.astype(F32))
     to_send(3)
     grad_4 = send(gsend.at[3], grecv.at[3], me.chip(-2))
-    to_row(0)
-    for item in in_row[6:9]:
-        to_sibling(*item)
+    weight_row(1)
     backward_a(0)
-    to_row(1)
-    for item in in_row[9:]:
-        to_sibling(*item)
 
     def finish_dq(c, _):
         dq_ref[pl.ds(c * CHUNK, CHUNK), :] = (dqt[c] * SCALE).T.astype(BF16)
@@ -321,7 +348,9 @@
     lax.fori_loop(0, CHUNKS, finish_dq, 0)
     add(0, (1 - core).astype(F32))
     to_row(2)
+    weight_row(2)
     to_row(3)
+    weight_row(3)
     grad_2.wait_recv()
     grad_4.wait_recv()
     add(2, 1.0)
@@ -342,15 +371,22 @@
                 ],
                 axis=1,
             )
-            lhs = jnp.concatenate([att[head, h] for h in range(HEADS)], axis=1)
+            lhs = jnp.concatenate(
+                [
+                    jnp.concatenate([att[head, c, h] for c in range(CHUNKS)], axis=0)
+                    for h in range(HEADS)
+                ],
+                axis=1,
+            )
             term = nt(lhs, rhs)
             total = term if total is None else total + term
     out_ref[...] = total.astype(BF16)
     for copy in started:
         copy.wait_send()
-
-
-SENDS = 100
+    assert len(started) == SENDS
+
+
+SENDS = 73
 
 
 def local(block_order, query_b, key_b, value_b, out_weight, query_a, key_a, value_a, grad_a):
@@ -365,29 +401,37 @@
             jax.ShapeDtypeStruct((ROWS, DIM), BF16),
             jax.ShapeDtypeStruct((ROWS, DIM), BF16),
         ),
-        in_specs=[pl.BlockSpec(memory_space=pltpu.SMEM)] + [vmem] * 8,
+        in_specs=[pl.BlockSpec(memory_space=pltpu.SMEM)] + [pl.BlockSpec(memory_space=pl.ANY)] * 8,
         out_specs=(vmem,) * 4,
         scratch_shapes=[
+            pltpu.VMEM((QROWS, DIM), BF16),
+            pltpu.VMEM((QROWS, DIM), BF16),
+            pltpu.VMEM((QROWS, DIM), BF16),
             pltpu.VMEM((5, 2, ROWS, DIM), BF16),
             pltpu.VMEM((5, 2, ROWS, DIM), BF16),
             pltpu.VMEM((2, Y, 4, 2, HEADS, 64, DIM), BF16),
-            pltpu.VMEM((8, HEADS, ROWS, DIM), BF16),
+            pltpu.VMEM((8, CHUNKS, HEADS, CHUNK // HEADS, DIM), BF16),
             pltpu.VMEM((5, CHUNKS, ROWS, CHUNK), F32),
             pltpu.VMEM((5, CHUNKS, ROWS, CHUNK), F32),
-            pltpu.VMEM((QROWS, DIM), F32),
+            pltpu.VMEM((CHUNK, DIM), F32),
             pltpu.VMEM((CHUNKS, DIM, CHUNK), F32),
             pltpu.VMEM((CHUNKS, DIM, CHUNK), F32),
             pltpu.VMEM((CHUNKS, 1, CHUNK), F32),
             pltpu.VMEM((CHUNKS, 1, CHUNK), F32),
             pltpu.VMEM((CHUNKS, 1, CHUNK), F32),
+            pltpu.VMEM((CHUNKS, 1, CHUNK), F32),
+            pltpu.VMEM((CHUNKS, 1, CHUNK), F32),
+            pltpu.VMEM((5, DIM, ROWS), BF16),
+            pltpu.VMEM((5, CHUNKS, ROWS, CHUNK), F32),
             pltpu.VMEM((2, ROWS, DIM), F32),
             pltpu.VMEM((4, 2, ROWS, DIM), BF16),
             pltpu.VMEM((4, 2, ROWS, DIM), BF16),
             pltpu.SemaphoreType.DMA((SENDS,)),
             pltpu.SemaphoreType.DMA((SENDS,)),
+            pltpu.SemaphoreType.DMA((7,)),
         ],
         compiler_params=pltpu.CompilerParams(
-            collective_id=0, has_side_effects=True, vmem_limit_bytes=48 * 2**20
+            collective_id=0, has_side_effects=True, vmem_limit_bytes=62 * 2**20
         ),
         name="attention",
     )(

time: 109 us -> 91.3 us (0.84)
  Pallas kernels: 98 us -> 84.9 us
  local copies, waits for them, and re-layouts: 9.7 us -> 4.07 us
    pallas_call x1, Pallas kernels: 98 us -> 84.9 us  [local(): pl.pallas_call(kernel, out_shape=(jax.ShapeDtypeStruct((ROWS, 512), BF16)...]
    unnamed x20 -> x10, local copies, waits for them, and re-layouts: 9.7 us -> 4.07 us
where the time goes in v2:
time: 91.3 us; the launch traced here: 90.3 us
  Pallas kernels  84.9 us (93%)
  local copies, waits for them, and re-layouts  4.07 us (4%)
  between operations  1.3 us (1%)
    pallas_call x1, Pallas kernels, local(): pl.pallas_call(kernel, out_shape=(jax.ShapeDtypeStruct((ROWS, 512), BF16)...  84.9 us
    unnamed x10, local copies, waits for them, and re-layouts  4.07 us

profile of v2, /device:TPU:1, one launch (start us, length us, event | category | flops | bytes accessed | tf_op | source)
XLA Modules:
  0.0 90.3 jit_solution(17604569177758242047)
XLA Ops:
  1.3 84.9 %attention.1 = (bf16[256,512]{1,0:T(8,128)(2,1)}, bf16[1024,128]{1,0:T(8,128)(2,1)}, bf16[256,128]{1,0:T(8,128)(2,1)}, bf16[256,128]{1,0:T(8,128)(2,1)}) custom-call(s32[1]{0:T(128)S(6)} %copy.17.order_ref, bf16[1024,128]{1,0:T(8,128)(2,1)} %bitcast.12, bf16[256,128]{1,0:T(8,128)(2,1)} %bitcast.15, bf16[256,128]{1,0:T(8,128)(2,1)} %bitcast.16, ...), custom_call_target="tpu_custom_call" | custom-call | tf_op jit(solution)/shard_map/attention/pallas_call | solution.py:396
  86.2 0.0 copy-start
  86.2 1.7 %copy.18 = bf16[256,512]{1,0:T(8,128)(2,1)} copy(bf16[256,512]{1,0:T(8,128)(2,1)} %get-tuple-element.16) | data formatting | bytes 524288
  87.9 0.0 copy-done
  87.9 0.0 copy-start.2
  87.9 0.7 copy.19
  88.6 0.2 copy-done.2
  88.8 0.0 copy-start.1
  88.8 0.6 copy.20
  89.4 0.2 copy-done.1
  89.7 0.6 copy.21
Async XLA Ops:
  86.2 1.7 %copy-start = (bf16[1024,128]{1,0:T(8,128)(2,1)S(1)}, bf16[1024,128]{1,0:T(8,128)(2,1)}, u32[]{:S(2)}) copy-start(bf16[1024,128]{1,0:T(8,128)(2,1)} %get-tuple-element.9) | copy-start | bytes 786436
  87.9 0.9 copy-start.2
  88.8 0.9 copy-start.1

commit v3 on v2

--- a/solution.py
+++ b/solution.py
@@ -76,7 +76,7 @@
     out_ref, dq_ref, dk_ref, dv_ref,
     qb_ref, qa_ref, ga_ref,
     kv_b, kv_a, wt, att, s_buf, dp_buf, rows_buf, acc, dqt, m_buf, l_buf, d_buf, mb_buf, lb_buf, vt_buf, sa_buf,
-    dkv, gsend, grecv, send_sem, recv_sem, load_sem,
+    dkv, gsend, grecv, send_sem, recv_sem, shared_sem, load_sem, even_sem, far_sem,
 ):
     me = Place(lax.axis_index("ctx"), lax.axis_index("head"))
     core = me.core
@@ -104,15 +104,29 @@
 
     started = []
 
-    def send(src, dst, target):
-        at = len(started)
+    taken = [0, 0]
+
+    def own_sem(sems, side):
+        taken[side] += 1
+        return sems.at[taken[side] - 1]
+
+    def send(src, dst, target, send_on=None, recv_on=None):
         copy = pltpu.make_async_remote_copy(
-            src_ref=src, dst_ref=dst, send_sem=send_sem.at[at], recv_sem=recv_sem.at[at],
+            src_ref=src, dst_ref=dst,
+            send_sem=own_sem(send_sem, 0) if send_on is None else shared_sem.at[send_on],
+            recv_sem=own_sem(recv_sem, 1) if recv_on is None else shared_sem.at[recv_on],
             device_id=target, device_id_type=MESH,
         )
         copy.start()
-        started.append(copy)
+        if send_on is None:
+            started.append(copy)
         return copy
+
+    def all_of(ref, send_on, recv_on):
+        return pltpu.make_async_remote_copy(
+            src_ref=ref, dst_ref=ref, send_sem=shared_sem.at[send_on],
+            recv_sem=shared_sem.at[recv_on], device_id=me.sibling(), device_id_type=MESH,
+        )
 
     def masked(s, hop, c):
         if hop not in (0, HOPS):
@@ -225,15 +239,37 @@
     forward_a(0)
     pl.semaphore_wait(barrier, len(sources))
 
-    def halo_first(kv):
+    even_chip = me.y % 2 == 0
+    from_even = []
+
+    class EvenOnly:
+        def __init__(self, src, dst, target, recv):
+            self.copy = pltpu.make_async_remote_copy(
+                src_ref=src, dst_ref=dst, send_sem=even_sem.at[len(from_even)], recv_sem=recv,
+                device_id=target, device_id_type=MESH,
+            )
+            pl.when(even_chip)(self.copy.start)
+            from_even.append(self.copy)
+
+        def wait_recv(self):
+            self.copy.wait_recv()
+
+    def halo_direct(kv):
         return [send(kv.at[0], kv.at[2 * by], me.chip(by)) for by in (1, 2)]
 
-    halo_b = halo_first(kv_b)
+    def halo_first(kv, at):
+        first = send(kv.at[0], kv.at[2], me.chip(1))
+        return [first, EvenOnly(kv.at[0], kv.at[4], me.chip(2), far_sem.at[at])]
+
+    def hand_on(kv, at):
+        return EvenOnly(kv.at[2], kv.at[4], me.chip(1), far_sem.at[at])
+
+    halo_b = halo_direct(kv_b)
     turn = [
         send(w_ref, wt.at[core, me.y, (me.head + 1) % 4, (me.head + 1) % Z // 4], me.turned(by))
         for by in (1, 5)
     ]
-    halo_a = halo_first(kv_a)
+    halo_a = halo_first(kv_a, 1)
 
     halo_b[0].wait_recv()
     rest_b = [send(kv_b.at[2 * core], kv_b.at[1], me.sibling())]
@@ -248,12 +284,12 @@
         vt_buf[hop] = kv_b[hop, 1].T
 
     own = me.z % 4
-    in_quad, in_row, in_chip = [], [], []
+    in_quad, in_row = [], []
 
     def spread(q):
         pair = wt.at[core, me.y, q]
-        got = [send(pair, pair, me.along_y(by)) for by in (1, 3, 2)]
-        in_chip.append(send(pair, pair, me.sibling()))
+        got = [send(pair, pair, me.along_y(by), send_on=2) for by in (1, 3, 2)]
+        send(pair, pair, me.sibling(), send_on=1, recv_on=0)
         in_row.append([(copy, by, q) for copy, by in zip(got, (1, 3, 2))])
 
     def weight_turned():
@@ -272,9 +308,9 @@
         for copy, by, q in in_row[at]:
             copy.wait_recv()
             pair = wt.at[core, (me.y - by + Y) % Y, q]
-            in_chip.append(send(pair, pair, me.sibling()))
-
-    across, beside, passed = [], [], []
+            send(pair, pair, me.sibling(), send_on=1, recv_on=0)
+
+    across = []
     for c in range(CHUNKS):
         rest_of_b(c)
         if c == 0:
@@ -282,15 +318,16 @@
         mine = att.at[me.head, c]
         across.append(send(mine, mine, me.other_half()))
         for by in (1, 3, 2):
-            beside.append(send(mine, mine, me.along_x(by)))
+            send(mine, mine, me.along_x(by), send_on=4, recv_on=3)
 
     def to_row(c):
         across[c].wait_recv()
         theirs = att.at[me.head + 1 - 2 * me.half, c]
         for by in (1, 3, 2):
-            passed.append(send(theirs, theirs, me.along_x(by)))
+            send(theirs, theirs, me.along_x(by), send_on=4, recv_on=3)
 
     halo_a[0].wait_recv()
+    hand_on(kv_a, 1)
     rest_a = [send(kv_a.at[2 * core], kv_a.at[1], me.sibling())]
     forward_a(2)
     halo_a[1].wait_recv()
@@ -358,8 +395,10 @@
     dk_ref[...] = (dkv[0] * SCALE).astype(BF16)
     dv_ref[...] = dkv[1].astype(BF16)
 
-    for copy in beside + in_chip + passed:
-        copy.wait_recv()
+    in_chip = all_of(wt.at[1 - core], 1, 0)
+    in_head = all_of(att.at[pl.ds(0, 6)], 4, 3)
+    in_chip.wait_recv()
+    in_head.wait_recv()
     total = None
     for q in range(4):
         for hi in range(2):
@@ -383,17 +422,40 @@
     out_ref[...] = total.astype(BF16)
     for copy in started:
         copy.wait_send()
-    assert len(started) == SENDS
-
-
-SENDS = 73
+    in_chip.wait_send()
+    in_head.wait_send()
+    all_of(wt.at[0, pl.ds(0, 3)], 2, 0).wait_send()
+
+    @pl.when(even_chip)
+    def _():
+        for copy in from_even:
+            copy.wait_send()
+
+    assert taken == [SENDS, RECVS], taken
+
+
+SENDS, RECVS = 20, 32
+
+
+def place(*refs):
+    ins, outs, held, sems = refs[:4], refs[4:8], refs[8:12], refs[12]
+    loads = [pltpu.make_async_copy(ins[i], held[i], sems.at[i]) for i in range(4)]
+    for load in loads:
+        load.start()
+    stores = []
+    for i in range(4):
+        loads[i].wait()
+        stores.append(pltpu.make_async_copy(held[i], outs[i], sems.at[4 + i]))
+        stores[i].start()
+    for store in stores:
+        store.wait()
 
 
 def local(block_order, query_b, key_b, value_b, out_weight, query_a, key_a, value_a, grad_a):
     flat_q = lambda a: a.reshape(QROWS, DIM)
     flat_k = lambda a: a.reshape(ROWS, DIM)
     vmem = pl.BlockSpec(memory_space=pltpu.VMEM)
-    out, dq, dk, dv = pl.pallas_call(
+    results = pl.pallas_call(
         kernel,
         out_shape=(
             jax.ShapeDtypeStruct((ROWS, 512), BF16),
@@ -427,8 +489,11 @@
             pltpu.VMEM((4, 2, ROWS, DIM), BF16),
             pltpu.VMEM((4, 2, ROWS, DIM), BF16),
             pltpu.SemaphoreType.DMA((SENDS,)),
-            pltpu.SemaphoreType.DMA((SENDS,)),
+            pltpu.SemaphoreType.DMA((RECVS,)),
+            pltpu.SemaphoreType.DMA((5,)),
             pltpu.SemaphoreType.DMA((7,)),
+            pltpu.SemaphoreType.DMA((2,)),
+            pltpu.SemaphoreType.DMA((2,)),
         ],
         compiler_params=pltpu.CompilerParams(
             collective_id=0, has_side_effects=True, vmem_limit_bytes=62 * 2**20
@@ -439,6 +504,17 @@
         jnp.transpose(out_weight, (0, 2, 1)),
         flat_q(query_a), flat_k(key_a), flat_k(value_a), flat_q(grad_a),
     )
+    shapes = tuple(jax.ShapeDtypeStruct(a.shape, a.dtype) for a in results)
+    out, dq, dk, dv = pl.pallas_call(
+        place,
+        out_shape=shapes,
+        in_specs=[pl.BlockSpec(memory_space=pl.ANY)] * 4,
+        out_specs=(pl.BlockSpec(memory_space=pl.ANY),) * 4,
+        scratch_shapes=[pltpu.VMEM(a.shape, a.dtype) for a in results]
+        + [pltpu.SemaphoreType.DMA((8,))],
+        compiler_params=pltpu.CompilerParams(vmem_limit_bytes=62 * 2**20),
+        name="place",
+    )(*results)
     flat = (ROWS, 1, DIM)
     return out, dq.reshape(ROWS, HEADS, DIM), dk.reshape(flat), dv.reshape(flat)
 

time: 91.3 us -> 87.7 us (0.961)
  local copies, waits for them, and re-layouts: 4.07 us -> 0 us
  Pallas kernels: 84.9 us -> 85.9 us
    unnamed x10 -> x0, local copies, waits for them, and re-layouts: 4.07 us -> none
    pallas_call x0 -> x1, Pallas kernels: none -> 1.84 us  [local(): pl.pallas_call(place, out_shape=shapes, in_specs=[pl.BlockSpec(memory_spa...]
where the time goes in v3:
time: 87.7 us; the launch traced here: 87.2 us
  Pallas kernels  85.9 us (98%)
  between operations  1.29 us (1%)
    pallas_call x1, Pallas kernels, local(): pl.pallas_call(kernel, out_shape=(jax.ShapeDtypeStruct((ROWS, 512), BF16)...  84.1 us
    pallas_call x1, Pallas kernels, local(): pl.pallas_call(place, out_shape=shapes, in_specs=[pl.BlockSpec(memory_spa...  1.84 us

profile of v3, /device:TPU:1, one launch (start us, length us, event | category | flops | bytes accessed | tf_op | source)
XLA Modules:
  0.0 87.2 jit_solution(15172595272596258280)
XLA Ops:
  1.3 84.1 %attention.1 = (bf16[256,512]{1,0:T(8,128)(2,1)}, bf16[1024,128]{1,0:T(8,128)(2,1)}, bf16[256,128]{1,0:T(8,128)(2,1)}, bf16[256,128]{1,0:T(8,128)(2,1)}) custom-call(s32[1]{0:T(128)S(6)} %copy.13.order_ref, bf16[1024,128]{1,0:T(8,128)(2,1)} %bitcast.11, bf16[256,128]{1,0:T(8,128)(2,1)} %bitcast.14, bf16[256,128]{1,0:T(8,128)(2,1)} %bitcast.15, ...), custom_call_target="tpu_custom_call" | custom-call | tf_op jit(solution)/shard_map/attention/pallas_call | solution.py:458
  85.4 1.8 %place.1 = (bf16[256,512]{1,0:T(8,128)(2,1)}, bf16[1024,128]{1,0:T(8,128)(2,1)}, bf16[256,128]{1,0:T(8,128)(2,1)}, bf16[256,128]{1,0:T(8,128)(2,1)}) custom-call(bf16[256,512]{1,0:T(8,128)(2,1)} %get-tuple-element.12.refs_0_, bf16[1024,128]{1,0:T(8,128)(2,1)} %get-tuple-element.13.refs_1_, bf16[256,128]{1,0:T(8,128)(2,1)} %get-tuple-element.14.refs_2_, ...), custom_call_target="tpu_custom_call" | custom-call | tf_op jit(solution)/shard_map/place/pallas_call | solution.py:508

commit v4 on v3

--- a/solution.py
+++ b/solution.py
@@ -73,7 +73,8 @@
 
 def kernel(
     order_ref, qb_hbm, kb_hbm, vb_hbm, w_ref, qa_hbm, ka_hbm, va_hbm, ga_hbm,
-    out_ref, dq_ref, dk_ref, dv_ref,
+    out_ref, dq_hbm, dk_hbm, dv_hbm,
+    dq_ref, dk_ref, dv_ref,
     qb_ref, qa_ref, ga_ref,
     kv_b, kv_a, wt, att, s_buf, dp_buf, rows_buf, acc, dqt, m_buf, l_buf, d_buf, mb_buf, lb_buf, vt_buf, sa_buf,
     dkv, gsend, grecv, send_sem, recv_sem, shared_sem, load_sem, even_sem, far_sem,
@@ -312,9 +313,9 @@
 
     across = []
     for c in range(CHUNKS):
-        rest_of_b(c)
         if c == 0:
             weight_turned()
+        rest_of_b(c)
         mine = att.at[me.head, c]
         across.append(send(mine, mine, me.other_half()))
         for by in (1, 3, 2):
@@ -383,6 +384,8 @@
         return 0
 
     lax.fori_loop(0, CHUNKS, finish_dq, 0)
+    stores = [pltpu.make_async_copy(dq_ref, dq_hbm, load_sem.at[7])]
+    stores[0].start()
     add(0, (1 - core).astype(F32))
     to_row(2)
     weight_row(2)
@@ -394,6 +397,10 @@
     add(3, 1.0)
     dk_ref[...] = (dkv[0] * SCALE).astype(BF16)
     dv_ref[...] = dkv[1].astype(BF16)
+    stores.append(pltpu.make_async_copy(dk_ref, dk_hbm, load_sem.at[8]))
+    stores.append(pltpu.make_async_copy(dv_ref, dv_hbm, load_sem.at[9]))
+    stores[1].start()
+    stores[2].start()
 
     in_chip = all_of(wt.at[1 - core], 1, 0)
     in_head = all_of(att.at[pl.ds(0, 6)], 4, 3)
@@ -420,6 +427,8 @@
             term = nt(lhs, rhs)
             total = term if total is None else total + term
     out_ref[...] = total.astype(BF16)
+    for store in stores:
+        store.wait()
     for copy in started:
         copy.wait_send()
     in_chip.wait_send()
@@ -464,8 +473,11 @@
             jax.ShapeDtypeStruct((ROWS, DIM), BF16),
         ),
         in_specs=[pl.BlockSpec(memory_space=pltpu.SMEM)] + [pl.BlockSpec(memory_space=pl.ANY)] * 8,
-        out_specs=(vmem,) * 4,
+        out_specs=(vmem,) + (pl.BlockSpec(memory_space=pl.ANY),) * 3,
         scratch_shapes=[
+            pltpu.VMEM((QROWS, DIM), BF16),
+            pltpu.VMEM((ROWS, DIM), BF16),
+            pltpu.VMEM((ROWS, DIM), BF16),
             pltpu.VMEM((QROWS, DIM), BF16),
             pltpu.VMEM((QROWS, DIM), BF16),
             pltpu.VMEM((QROWS, DIM), BF16),
@@ -491,7 +503,7 @@
             pltpu.SemaphoreType.DMA((SENDS,)),
             pltpu.SemaphoreType.DMA((RECVS,)),
             pltpu.SemaphoreType.DMA((5,)),
-            pltpu.SemaphoreType.DMA((7,)),
+            pltpu.SemaphoreType.DMA((10,)),
             pltpu.SemaphoreType.DMA((2,)),
             pltpu.SemaphoreType.DMA((2,)),
         ],

time: 87.7 us -> 87 us (level)
  no operation moved by 1% of the time
where the time goes in v4:
time: 87 us; the launch traced here: 86.5 us
  Pallas kernels  85.2 us (98%)
  between operations  1.29 us (1%)
    pallas_call x1, Pallas kernels, local(): pl.pallas_call(kernel, out_shape=(jax.ShapeDtypeStruct((ROWS, 512), BF16)...  83.3 us
    pallas_call x1, Pallas kernels, local(): pl.pallas_call(place, out_shape=shapes, in_specs=[pl.BlockSpec(memory_spa...  1.84 us

profile of v4, /device:TPU:1, one launch (start us, length us, event | category | flops | bytes accessed | tf_op | source)
XLA Modules:
  0.0 86.5 jit_solution(4168153525949107212)
XLA Ops:
  1.3 83.3 %attention.1 = (bf16[256,512]{1,0:T(8,128)(2,1)}, bf16[1024,128]{1,0:T(8,128)(2,1)}, bf16[256,128]{1,0:T(8,128)(2,1)}, bf16[256,128]{1,0:T(8,128)(2,1)}) custom-call(s32[1]{0:T(128)S(6)} %copy.13.order_ref, bf16[1024,128]{1,0:T(8,128)(2,1)} %bitcast.11, bf16[256,128]{1,0:T(8,128)(2,1)} %bitcast.14, bf16[256,128]{1,0:T(8,128)(2,1)} %bitcast.15, ...), custom_call_target="tpu_custom_call" | custom-call | tf_op jit(solution)/shard_map/attention/pallas_call | solution.py:467
  84.6 1.8 %place.1 = (bf16[256,512]{1,0:T(8,128)(2,1)}, bf16[1024,128]{1,0:T(8,128)(2,1)}, bf16[256,128]{1,0:T(8,128)(2,1)}, bf16[256,128]{1,0:T(8,128)(2,1)}) custom-call(bf16[256,512]{1,0:T(8,128)(2,1)} %get-tuple-element.12.refs_0_, bf16[1024,128]{1,0:T(8,128)(2,1)} %get-tuple-element.13.refs_1_, bf16[256,128]{1,0:T(8,128)(2,1)} %get-tuple-element.14.refs_2_, ...), custom_call_target="tpu_custom_call" | custom-call | tf_op jit(solution)/shard_map/place/pallas_call | solution.py:520
